TPU v7x, 256 devices: a whole 4x4x8 slice. The times are simulated.
256 devices in a mesh: resp: 32 (over x, z), kvh: 8 (over y, core).
Axes of the slice: x: 4, y: 4, z: 8, core: 2. Of those that a mesh axis runs over, the one named last changes fastest.
Arguments:
- query: bfloat16 [32, 256, 8192], P('resp', None, 'kvh'), may hold values from -8 to 8
- output_gradient: bfloat16 [32, 256, 8192], P('resp', None, 'kvh'), may hold values from -6 to 6
- prompt_key_pool: bfloat16 [128, 128, 1024], P('resp', 'kvh'), may hold values from -8 to 8
- prompt_value_pool: bfloat16 [128, 128, 1024], P('resp', 'kvh'), may hold values from -6 to 6
- block_tables: int32 [32, 16], replicated, may hold values from 0 to 127, as said below
- lengths: int32 [32], P('resp'), may hold values from 32 to 256, as said below
Outputs:
- grad_query: bfloat16 [32, 256, 8192], P('resp', None, 'kvh')
- grad_key: float32 [128, 128, 1024], P('resp', 'kvh')
- grad_value: float32 [128, 128, 1024], P('resp', 'kvh')
Inputs may be any that keep to these rules, and one draw needn't show every extreme that they name: `block_tables`: response r reads the pages of prompt r // 16: all 16 responses of a prompt have the same table. A table names 16 distinct pages; pool page p is owned by index p // 4 of resp, and the pages of a table lie on 8 owners with exactly 2 on each. `lengths`: some response has all 256 tokens live.
All inputs are finite; a program needn't handle non-finite values.
Results may differ from a plain program's by a relative error of at most 0.011.
Values may be sent and summed in bfloat16 or wider, within the bound.
A program may use at most 128 MiB of HBM per device.

v0:
```python
import jax
import jax.numpy as jnp
from jax import lax
from jax.sharding import PartitionSpec as P

QUERY_HEADS = 64
KEY_VALUE_HEADS = 8
HEAD_WIDTH = 128


def head_gradients(query_rows, upstream_gradient, live_rows, paged_keys, paged_values, score_scale):
    row_count = query_rows.shape[0]
    block_rows = min(512, row_count)
    blocks = row_count // block_rows
    key_row_block = paged_keys.shape[0]
    head_size = paged_keys.shape[1]
    contract_cols = (((1,), (1,)), ((), ()))
    contract_rows = (((0,), (0,)), ((), ()))

    def one_block(totals, pieces):
        key_gradient, value_gradient = totals
        query_block, upstream_block, live_block = pieces
        scores = (
            lax.dot_general(
                query_block, paged_keys, contract_cols, preferred_element_type=jnp.float32
            )
            * score_scale
        )
        attention = jax.nn.softmax(scores, axis=-1)
        grad_attn = lax.dot_general(
            upstream_block, paged_values, contract_cols, preferred_element_type=jnp.float32
        )
        delta_rows = jnp.sum(attention * grad_attn, axis=-1, keepdims=True)
        grad_scores = attention * (grad_attn - delta_rows)
        attention_b = jnp.where(live_block[:, None], attention, 0.0).astype(jnp.bfloat16)
        scores_b = jnp.where(live_block[:, None], grad_scores, 0.0).astype(jnp.bfloat16)
        grad_queries = (
            jnp.dot(scores_b, paged_keys, preferred_element_type=jnp.float32) * score_scale
        ).astype(jnp.bfloat16)
        key_gradient = (
            key_gradient
            + lax.dot_general(
                scores_b, query_block, contract_rows, preferred_element_type=jnp.float32
            )
            * score_scale
        )
        value_gradient = value_gradient + lax.dot_general(
            attention_b, upstream_block, contract_rows, preferred_element_type=jnp.float32
        )
        return ((key_gradient, value_gradient), grad_queries)

    zero_filled = jnp.zeros((key_row_block, head_size), jnp.float32)
    pieces = (
        query_rows.reshape(blocks, block_rows, head_size),
        upstream_gradient.reshape(blocks, block_rows, head_size),
        live_rows.reshape(blocks, block_rows),
    )
    (key_gradient, value_gradient), grad_queries = lax.scan(
        one_block, (zero_filled, zero_filled), pieces
    )
    return (grad_queries.reshape(row_count, head_size), key_gradient, value_gradient)


def shards(query, output_gradient, prompt_key_pool, prompt_value_pool, block_tables, lengths):
    resp_count = lax.axis_size("resp")
    own_index = lax.axis_index("resp")
    pages_dev = prompt_key_pool.shape[0]
    head_keys, head_values = (
        lax.all_to_all(prompt_key_pool, "kvh", split_axis=2, concat_axis=1, tiled=True),
        lax.all_to_all(prompt_value_pool, "kvh", split_axis=2, concat_axis=1, tiled=True),
    )
    page_tok = head_keys.shape[1]
    columns = head_keys.shape[2]
    page_count = block_tables.shape[1]
    response_table = lax.dynamic_index_in_dim(block_tables, own_index, 0, keepdims=False)
    all_keys, all_values = (
        lax.all_gather(head_keys, "resp", axis=0, tiled=True),
        lax.all_gather(head_values, "resp", axis=0, tiled=True),
    )
    paged_keys = all_keys[response_table]
    paged_values = all_values[response_table]
    key_row_block = page_count * page_tok
    paged_keys = paged_keys.reshape(key_row_block, columns)
    paged_values = paged_values.reshape(key_row_block, columns)
    kv_local = columns // HEAD_WIDTH
    group_width = QUERY_HEADS // KEY_VALUE_HEADS
    token_count = query.shape[1]
    score_scale = HEAD_WIDTH ** (-0.5)
    query_rows = query[0].reshape(token_count, kv_local, group_width, HEAD_WIDTH)
    upstream_gradient = output_gradient[0].reshape(token_count, kv_local, group_width, HEAD_WIDTH)
    live_rows = jnp.repeat(jnp.arange(token_count) < lengths[0], group_width)
    grad_queries, key_gradient, value_gradient = head_gradients(
        query_rows[:, 0].reshape(token_count * group_width, HEAD_WIDTH),
        upstream_gradient[:, 0].reshape(token_count * group_width, HEAD_WIDTH),
        live_rows,
        paged_keys,
        paged_values,
        score_scale,
    )
    query_parts = grad_queries.reshape(token_count, 1, group_width, HEAD_WIDTH)
    grad_query = query_parts.reshape(1, token_count, kv_local * group_width * HEAD_WIDTH)
    key_pages = key_gradient.reshape(page_count, page_tok, columns)
    value_pages = value_gradient.reshape(page_count, page_tok, columns)
    pool_zero = jnp.zeros((resp_count * pages_dev, page_tok, columns), jnp.float32)
    full_keys = pool_zero.at[response_table].add(key_pages)
    full_values = pool_zero.at[response_table].add(value_pages)
    summed_keys, summed_values = (
        lax.psum_scatter(full_keys, "resp", scatter_dimension=0, tiled=True),
        lax.psum_scatter(full_values, "resp", scatter_dimension=0, tiled=True),
    )
    grad_key, grad_value = (
        lax.all_to_all(summed_keys, "kvh", split_axis=1, concat_axis=2, tiled=True),
        lax.all_to_all(summed_values, "kvh", split_axis=1, concat_axis=2, tiled=True),
    )
    return (grad_query, grad_key, grad_value)


def solution(mesh):
    placed = (
        P("resp", None, "kvh"),
        P("resp", None, "kvh"),
        P("resp", "kvh", None),
        P("resp", "kvh", None),
        P(),
        P("resp"),
    )
    return jax.shard_map(
        shards,
        mesh=mesh,
        in_specs=placed,
        out_specs=(P("resp", None, "kvh"), P("resp", "kvh", None), P("resp", "kvh", None)),
        check_vma=False,
    )
```

profile of v0, /device:TPU:1, one launch (start us, length us, event | category | flops | bytes accessed | tf_op | source)
XLA Modules:
  0.0 714.5 jit_solution(1627153024784739608)
XLA Ops:
  7.2 1.5 copy.23
  8.8 1.1 reshape.92
  9.9 11.2 %all_to_all.72 = bf16[8,2,4096]{2,1,0:T(2,128)(2,1)S(1)} all-to-all(bf16[8,2,4096]{2,1,0:T(2,128)(2,1)S(1)} %reshape.92), channel_id=1, replica_groups=mesh['resp'=32,'kvh'=8] {'kvh'}, dimensions={0} | all-to-all | bytes 262144 | tf_op jit(solution)/shard_map/all_to_all | solution.py:69
  21.0 0.7 reshape.93
  21.8 1.2 copy.36
  23.1 0.7 copy.26
  23.8 1.1 reshape.94
  24.8 8.5 %all_to_all.73 = bf16[8,2,4096]{2,1,0:T(2,128)(2,1)S(1)} all-to-all(bf16[8,2,4096]{2,1,0:T(2,128)(2,1)S(1)} %reshape.94), channel_id=1, replica_groups=mesh['resp'=32,'kvh'=8] {'kvh'}, dimensions={0} | all-to-all | bytes 262144 | tf_op jit(solution)/shard_map/all_to_all | solution.py:70
  33.3 0.7 reshape.95
  34.1 1.2 copy.38
  35.3 0.2 reduce-scatter.3.cloned.1.call-start
  36.2 0.1 broadcast_in_dim.47
  36.3 0.1 broadcast_in_dim.48
  36.5 0.2 reshape_reshape_squeeze_reshape_squeeze.6
  36.7 2.1 reshape_reshape_squeeze_reshape_squeeze.7
  38.8 0.2 dynamic-slice_reduce_fusion.1
  39.0 64.3 %all-gather.3.cloned.1.call-done = bf16[128,128,128]{2,1,0:T(8,128)(2,1)} async-done(((bf16[4,128,128]{2,1,0:T(8,128)(2,1)}), bf16[128,128,128]{2,1,0:T(8,128)(2,1)}) %all-gather.3.cloned.1.call-update) | async-done | bytes 4194320 | tf_op jit(solution)/shard_map/all_gather | solution.py:77
  103.4 2.8 gather_fusion
  106.2 79.4 %all-gather.5.cloned.1.call-done = bf16[128,128,128]{2,1,0:T(8,128)(2,1)} async-done(((bf16[4,128,128]{2,1,0:T(8,128)(2,1)}), bf16[128,128,128]{2,1,0:T(8,128)(2,1)}) %all-gather.5.cloned.1.call-update) | async-done | bytes 4194320 | tf_op jit(solution)/shard_map/all_gather | solution.py:78
  185.6 3.6 gather_fusion.1
  189.2 36.5 %while.15 = (s32[]{:T(128)}, f32[2048,128]{1,0:T(8,128)S(1)}, f32[2048,128]{1,0:T(8,128)S(1)}, bf16[4,512,128]{2,1,0:T(8,128)(2,1)}, pred[4,512]{1,0:T(4,128)(4,...) while((s32[]{:T(128)}, f32[2048,128]{1,0:T(8,128)S(1)}, ...), condition=%wide.region_4.5_spmd.clone, body=%wide.region_0.4_spmd.clone.sunk | while | flops 1366686208 | bytes 46293196 | solution.py:58
  189.2 0.8 multiply_reduce_fusion.4
  190.0 0.8 fusion.47
  190.8 1.9 convolution_add_fusion.2
  192.8 1.6 multiply_reduce_fusion.5
  194.3 1.5 select_convert_fusion.6
  195.9 1.4 fusion.49
  197.2 1.1 fusion.48
  198.3 0.8 multiply_reduce_fusion.4
  199.1 0.8 fusion.47
  200.0 1.9 convolution_add_fusion.2
  201.9 1.6 multiply_reduce_fusion.5
  203.5 1.5 select_convert_fusion.6
  205.0 1.4 fusion.49
  206.4 1.1 fusion.48
  207.5 0.8 multiply_reduce_fusion.4
  208.3 0.8 fusion.47
  209.1 1.9 convolution_add_fusion.2
  211.0 1.6 multiply_reduce_fusion.5
  212.6 1.5 select_convert_fusion.6
  214.1 1.4 fusion.49
  215.5 1.1 fusion.48
  216.6 0.8 multiply_reduce_fusion.4
  217.4 0.8 fusion.47
  218.3 1.9 convolution_add_fusion.2
  220.2 1.6 multiply_reduce_fusion.5
  221.8 1.5 select_convert_fusion.6
  223.3 1.4 fusion.49
  224.6 1.1 fusion.48
  225.7 4.3 broadcast_in_dim.49.clone
  230.0 3.4 scatter_fusion
  233.4 0.0 reduce-scatter.5.cloned.1.call-start
  233.5 4.3 broadcast_in_dim.49.clone.1
  237.8 3.4 scatter_fusion.1
  241.2 217.0 %reduce-scatter.3.cloned.1.call-done = f32[4,128,128]{2,1,0:T(8,128)} async-done(((f32[128,128,128]{2,1,0:T(8,128)}), f32[4,128,128]{2,1,0:T(8,128)}) %reduce-scatter.3.cloned.1.call-update) | async-done | bytes 262160 | tf_op jit(solution)/shard_map/reduce_scatter | solution.py:108
  458.3 1.8 copy.29
  460.1 8.8 %all-to-all-start.2 = ((f32[4,128,128]{2,0,1:T(4,128)}), f32[4,128,128]{2,0,1:T(4,128)S(1)}, u32[]{:S(2)}, u32[]{:S(2)}) async-start(f32[4,128,128]{2,0,1:T(4,128)} %copy.29), calls=%async_computation.3 | async-start | bytes 524288 | tf_op jit(solution)/shard_map/all_to_all | solution.py:112
  468.9 221.2 %reduce-scatter.5.cloned.1.call-done = f32[4,128,128]{2,1,0:T(8,128)} async-done(((f32[128,128,128]{2,1,0:T(8,128)}), f32[4,128,128]{2,1,0:T(8,128)}) %reduce-scatter.5.cloned.1.call-update) | async-done | bytes 262160 | tf_op jit(solution)/shard_map/reduce_scatter | solution.py:109
  690.1 1.8 copy.32
  691.9 8.8 %all-to-all-start.3 = ((f32[4,128,128]{2,0,1:T(4,128)}), f32[4,128,128]{2,0,1:T(4,128)S(1)}, u32[]{:S(2)}, u32[]{:S(2)}) async-start(f32[4,128,128]{2,0,1:T(4,128)} %copy.32), calls=%async_computation.5 | async-start | bytes 524288 | tf_op jit(solution)/shard_map/all_to_all | solution.py:113
  700.7 1.0 reshape_reshape_reshape.3
  701.8 0.7 copy.44
  702.5 4.7 all-to-all-done.3
  707.3 0.7 copy.43
  (43 shorter events, 0.4 us)
Async XLA Ops:
  7.2 31.7 %copy-start = (s32[32,16]{0,1:T(8,128)S(1)}, s32[32,16]{0,1:T(8,128)}, u32[]{:S(2)}) copy-start(s32[32,16]{0,1:T(8,128)} %param.12) | copy-start | bytes 6148
  7.2 15.9 %copy-start.5 = (bf16[4,16,1024]{2,1,0:T(8,128)(2,1)S(1)}, bf16[4,16,1024]{2,1,0:T(8,128)(2,1)}, u32[]{:S(2)}) copy-start(bf16[4,16,1024]{2,1,0:T(8,128)(2,1)} %param.11) | copy-start | bytes 393220
  7.2 96.2 %all-gather.3.cloned.1.call-start = ((), (), s32[]{:S(2)}) async-start(), calls=%async_computation.6 | async-start | bytes 4325376 | tf_op jit(solution)/shard_map/all_gather | solution.py:77
  9.9 26.6 %copy-start.1 = (bf16[1,256,1024]{2,1,0:T(8,128)(2,1)S(1)}, bf16[1,256,1024]{2,1,0:T(8,128)(2,1)}, u32[]{:S(2)}) copy-start(bf16[1,256,1024]{2,1,0:T(8,128)(2,1)} %param.8) | copy-start | bytes 1572868
  23.0 162.6 %all-gather.5.cloned.1.call-start = ((), (), s32[]{:S(2)}) async-start(), calls=%async_computation.7 | async-start | bytes 4325376 | tf_op jit(solution)/shard_map/all_gather | solution.py:78
  35.3 423.0 %reduce-scatter.3.cloned.1.call-start = ((), (), s32[]{:S(2)}) async-start(), calls=%async_computation.8 | async-start | bytes 8650752 | tf_op jit(solution)/shard_map/reduce_scatter | solution.py:108
  189.2 1.6 copy-start.2
  190.8 1.9 copy-start.4
  198.3 1.6 copy-start.2
  200.0 1.9 copy-start.4
  207.5 1.6 copy-start.2
  209.1 1.9 copy-start.4
  216.6 1.6 copy-start.2
  218.2 1.9 copy-start.4
  233.4 456.7 %reduce-scatter.5.cloned.1.call-start = ((), (), s32[]{:S(2)}) async-start(), calls=%async_computation.9 | async-start | bytes 8650752 | tf_op jit(solution)/shard_map/reduce_scatter | solution.py:109
  241.2 459.5 %copy-start.3 = (bf16[4,512,128]{2,1,0:T(8,128)(2,1)S(1)}, bf16[4,512,128]{2,1,0:T(8,128)(2,1)}, u32[]{:S(2)}) copy-start(bf16[4,512,128]{2,1,0:T(8,128)(2,1)} %get-tuple-element.52) | copy-start | bytes 1572868
  460.1 231.9 %all-to-all-start.2 = ((f32[4,128,128]{2,0,1:T(4,128)}), f32[4,128,128]{2,0,1:T(4,128)S(1)}, u32[]{:S(2)}, u32[]{:S(2)}) async-start(f32[4,128,128]{2,0,1:T(4,128)} %copy.29), calls=%async_computation.3 | async-start | bytes 524288 | tf_op jit(solution)/shard_map/all_to_all | solution.py:112
  691.9 15.3 %all-to-all-start.3 = ((f32[4,128,128]{2,0,1:T(4,128)}), f32[4,128,128]{2,0,1:T(4,128)S(1)}, u32[]{:S(2)}, u32[]{:S(2)}) async-start(f32[4,128,128]{2,0,1:T(4,128)} %copy.32), calls=%async_computation.5 | async-start | bytes 524288 | tf_op jit(solution)/shard_map/all_to_all | solution.py:113
Sparse Core Ops, SparseCore 0:
  23.1 80.2 all-gather.2
  106.5 79.0 all-gather.4
  233.6 224.6 reduce-scatter.2
  462.7 227.4 reduce-scatter.4
where the time goes:
time: 715 us
  waiting for transfers between devices  587 us (82%)
  local copies, waits for them, and re-layouts  32.2 us (5%)
  matrix products  26.8 us (4%)
  blocking collectives  19.7 us (3%)
  starting transfers between devices  18 us (3%)
  other arithmetic  16.2 us (2%)
  between operations  14.6 us (2%)
    reduce_scatter x1, waiting for transfers between devices, shards(): lax.psum_scatter(full_values, 'resp', scatter_dimension=0, tiled=True)  221 us
    reduce_scatter x1, waiting for transfers between devices, shards(): lax.psum_scatter(full_keys, 'resp', scatter_dimension=0, tiled=True)  217 us
    all_gather x1, waiting for transfers between devices, shards(): lax.all_gather(head_values, 'resp', axis=0, tiled=True)  79.4 us
    all_gather x1, waiting for transfers between devices, shards(): lax.all_gather(head_keys, 'resp', axis=0, tiled=True)  64.3 us
  transfers between devices with their start and end apart: 6, of which 5 were waited for; matrix products, arithmetic and copies ran while one was open for 3% of the time, Pallas kernels for 0%

commit v1 on v0

v1 whole, which is shorter than its diff:
```python
import functools

import jax
import jax.numpy as jnp
from jax import lax
from jax.experimental import pallas as pl
from jax.experimental.pallas import tpu as pltpu
from jax.sharding import PartitionSpec as P

QUERY_HEADS = 64
KEY_VALUE_HEADS = 8
HEAD_WIDTH = 128
PAGES_DEV = 4
SLOTS = 2
ROWS = 16
MESH = pl.DeviceIdType.MESH
LOG2E = 1.4426950408889634


def place():
    rings = lax.axis_size("kvh")
    own = lax.axis_index("resp")
    head = lax.axis_index("kvh")
    return own, head, own // rings, lax.rem(own, rings), rings


def mod(value, size):
    return lax.rem(value + 2 * size, size)


def local_slots(tables, prompt, own, share, pages):
    first, second, count = jnp.int32(-1), jnp.int32(-1), jnp.int32(0)
    for j in range(pages):
        page = tables[prompt * share, j]
        hit = (page // PAGES_DEV) == own
        local = lax.rem(page, PAGES_DEV)
        first = jnp.where(hit & (count == 0), local, first)
        second = jnp.where(hit & (count == 1), local, second)
        count = count + hit.astype(jnp.int32)
    return first, second


def prompt_owners(tables, prompt, share, pages):
    held = [tables[prompt * share, j] // PAGES_DEV for j in range(pages)]
    ranks = []
    for j in range(pages):
        below = jnp.int32(0)
        for i in range(pages):
            if i != j:
                below = below + (held[i] < held[j]).astype(jnp.int32)
        ranks.append(below // SLOTS)
    owners = []
    for n in range(pages // SLOTS):
        owner = jnp.int32(0)
        for j in range(pages):
            owner = jnp.where(ranks[j] == n, held[j], owner)
        owners.append(owner)
    return owners


def spread_peers(own_x, own_z, head, rings, x_count):
    def target(i):
        dx, dh = i // rings, lax.rem(i, rings)
        x = lax.rem(own_x + dx, x_count)
        h = lax.rem(head + dh, rings)
        z = mod(own_z - dh + 1, rings)
        return x, h, z

    def origin(i):
        dx, dk = i // rings, lax.rem(i, rings)
        x = lax.rem(own_x + dx, x_count)
        k = lax.rem(head + dk, rings)
        z = mod(own_z - dk - 1, rings)
        return x, k, z

    return target, origin


def ring_peers(own_x, own_z, rings):
    right = own_x * rings + lax.rem(own_z + 1, rings)
    left = own_x * rings + mod(own_z - 1, rings)
    buddy = (own_x + 1 - 2 * lax.rem(own_x, 2)) * rings + own_z
    return right, left, buddy


def gather_kernel(share, pages, tables, key_pool, value_pool, out, stage, recv,
                  spread_send, spread_recv, send_sem, recv_sem):
    own, head, own_x, own_z, rings = place()
    x_count = lax.axis_size("resp") // rings
    target, origin = spread_peers(own_x, own_z, head, rings, x_count)
    right, left, buddy = ring_peers(own_x, own_z, rings)
    messages = x_count * rings

    barrier = pltpu.get_barrier_semaphore()

    def greet(i, carry):
        x, k, z = origin(i)
        pl.semaphore_signal(barrier, inc=1, device_id=(x * rings + z, k), device_id_type=MESH)
        return carry

    lax.fori_loop(0, messages, greet, 0)
    for peer in (right, left, buddy):
        pl.semaphore_signal(barrier, inc=1, device_id=(peer, head), device_id_type=MESH)

    for prompt in range(x_count // 2):
        picked = local_slots(tables, prompt, own, share, pages)
        for slot in range(SLOTS):
            page = jnp.maximum(picked[slot], 0)
            for h in range(rings):
                columns = slice(h * HEAD_WIDTH, (h + 1) * HEAD_WIDTH)
                stage[prompt * SLOTS + slot, h, :ROWS, :] = key_pool[page, :, columns]
                stage[prompt * SLOTS + slot, h, ROWS:, :] = value_pool[page, :, columns]

    pl.semaphore_wait(barrier, messages + 3)

    def send(i, carry):
        x, h, z = target(i)
        pltpu.make_async_remote_copy(
            src_ref=stage.at[x, h], dst_ref=recv.at[own], send_sem=spread_send, recv_sem=spread_recv,
            device_id=(x * rings + z, h), device_id_type=MESH,
        ).start()
        return carry

    lax.fori_loop(0, messages, send, 0)
    owners = prompt_owners(tables, own_x // 2, share, pages)
    pltpu.make_async_copy(recv, recv, spread_recv).wait()

    side = lax.rem(own_x, 2)
    mine = side * rings + own_z
    for n, owner in enumerate(owners):
        piece = recv[owner]
        out[mine, 0, n * ROWS:(n + 1) * ROWS, :] = piece[:ROWS]
        out[mine, 1, n * ROWS:(n + 1) * ROWS, :] = piece[ROWS:]

    copies = []
    slot_of = {}

    def push(name, chunk, part, peer):
        slot = slot_of.setdefault(name, len(slot_of))
        copy = pltpu.make_async_remote_copy(
            src_ref=out.at[chunk, part], dst_ref=out.at[chunk, part],
            send_sem=send_sem.at[slot], recv_sem=recv_sem.at[slot],
            device_id=(peer, head), device_id_type=MESH,
        )
        copy.start()
        copies.append(copy)
        return copy

    other = (1 - side) * rings
    same = side * rings
    hops = {1: rings // 2, -1: rings // 2 - 1}
    peers = {1: right, -1: left}
    moving = {}
    moving["x", 1] = push(("x", 1), mine, 1, buddy)
    for way in (1, -1):
        for part in (0, 1):
            moving["z", way, 0, part, 0] = push(("z", way, 0, part, 0), mine, part, peers[way])
    moving["x", 0, 0] = push(("x", 0, 0), mine, 0, buddy)
    moving["x", 1].wait_recv()
    for way in (1, -1):
        moving["z", way, 0, 1, 1] = push(("z", way, 0, 1, 1), other + own_z, 1, peers[way])
    for step in range(1, rings // 2 + 1):
        for part, flip in ((0, 0), (1, 0), (1, 1)):
            for way in (1, -1):
                if step > hops[way]:
                    continue
                moving["z", way, step - 1, part, flip].wait_recv()
                chunk = (other if flip else same) + mod(own_z - way * step, rings)
                if step < hops[way]:
                    name = ("z", way, step, part, flip)
                    moving[name] = push(name, chunk, part, peers[way])
                if part == 0:
                    name = ("x", 0, way * step)
                    moving[name] = push(name, chunk, part, buddy)
    for name, copy in moving.items():
        if name[0] == "x" and name[1] == 0:
            copy.wait_recv()
    for copy in copies:
        copy.wait_send()
    pltpu.make_async_copy(stage, stage, spread_send).wait()


def gather_copies(rings):
    return 1 + rings + 3 * (rings - 1)


def gathered(tables, key_pool, value_pool, share, pages):
    rings = lax.axis_size("kvh")
    devices = lax.axis_size("resp")
    x_count = devices // rings
    rows = rings * ROWS
    return pl.pallas_call(
        functools.partial(gather_kernel, share, pages),
        out_shape=jax.ShapeDtypeStruct((SLOTS * rings, 2, rows, HEAD_WIDTH), jnp.bfloat16),
        in_specs=[
            pl.BlockSpec(memory_space=pltpu.SMEM),
            pl.BlockSpec(memory_space=pltpu.VMEM),
            pl.BlockSpec(memory_space=pltpu.VMEM),
        ],
        out_specs=pl.BlockSpec(memory_space=pltpu.VMEM),
        scratch_shapes=[
            pltpu.VMEM((x_count, rings, 2 * ROWS, HEAD_WIDTH), jnp.bfloat16),
            pltpu.VMEM((devices, 2 * ROWS, HEAD_WIDTH), jnp.bfloat16),
            pltpu.SemaphoreType.DMA,
            pltpu.SemaphoreType.DMA,
            pltpu.SemaphoreType.DMA((gather_copies(rings),)),
            pltpu.SemaphoreType.DMA((gather_copies(rings),)),
        ],
        compiler_params=pltpu.CompilerParams(
            collective_id=0, has_side_effects=True, vmem_limit_bytes=16 * 2**20
        ),
    )(tables, key_pool, value_pool)


def attention_kernel(chunk_rows, lengths, query, upstream, pages, grad_query, grad_pages,
                     keys_t, score, slope, soft):
    group = pl.program_id(0)
    chunks = pages.shape[0]
    tokens = query.shape[0]
    scale = HEAD_WIDTH ** -0.5
    rows_t = (((1,), (1,)), ((), ()))

    @pl.when(group == 0)
    def _():
        def turn(c, carry):
            keys_t[c] = pages[c, 0].T
            grad_pages[c] = jnp.zeros_like(grad_pages[c])
            return carry
        lax.fori_loop(0, chunks, turn, 0)

    query_t = query[...].T
    upstream_t = upstream[...].T

    def scores(c, top):
        part = jnp.dot(pages[c, 0], query_t, preferred_element_type=jnp.float32) * (scale * LOG2E)
        score[c] = part
        slope[c] = jnp.dot(pages[c, 1], upstream_t, preferred_element_type=jnp.float32)
        return jnp.maximum(top, jnp.max(part.reshape(-1, 8, tokens), axis=0))

    top = lax.fori_loop(0, chunks, scores, jnp.full((8, tokens), -jnp.inf, jnp.float32))
    top = jnp.max(top, axis=0, keepdims=True)

    def weights(c, carry):
        total, delta = carry
        part = jnp.exp2(score[c] - top)
        score[c] = part
        soft[c] = part.astype(jnp.bfloat16)
        total = total + jnp.sum(part.reshape(-1, 8, tokens), axis=0)
        delta = delta + jnp.sum((part * slope[c]).reshape(-1, 8, tokens), axis=0)
        return total, delta

    zero = jnp.zeros((8, tokens), jnp.float32)
    total, delta = lax.fori_loop(0, chunks, weights, (zero, zero))
    inverse = 1.0 / jnp.sum(total, axis=0, keepdims=True)
    delta = jnp.sum(delta, axis=0, keepdims=True) * inverse
    live = lax.broadcasted_iota(jnp.int32, (1, tokens), 1) < lengths[0]
    inverse = jnp.where(live, inverse, 0.0)
    query_s = (query_t.astype(jnp.float32) * (inverse * scale)).astype(jnp.bfloat16)
    upstream_s = (upstream_t.astype(jnp.float32) * inverse).astype(jnp.bfloat16)

    def gradients(c, total):
        slopes = (score[c] * (slope[c] - delta)).astype(jnp.bfloat16)
        grad_pages[c, 0] += lax.dot_general(slopes, query_s, rows_t, preferred_element_type=jnp.float32)
        grad_pages[c, 1] += lax.dot_general(soft[c], upstream_s, rows_t, preferred_element_type=jnp.float32)
        return total + jnp.dot(keys_t[c], slopes, preferred_element_type=jnp.float32)

    total = lax.fori_loop(0, chunks, gradients, jnp.zeros((HEAD_WIDTH, tokens), jnp.float32))
    grad_query[...] = (total * (inverse * scale)).T.astype(jnp.bfloat16)


def attention_gradients(lengths, query, upstream, pages):
    tokens, width = query.shape
    groups = width // HEAD_WIDTH
    chunks, _, rows, _ = pages.shape
    block = pl.BlockSpec((tokens, HEAD_WIDTH), lambda g: (0, g))
    whole = pl.BlockSpec(pages.shape, lambda g: (0, 0, 0, 0))
    return pl.pallas_call(
        functools.partial(attention_kernel, rows),
        grid=(groups,),
        out_shape=(
            jax.ShapeDtypeStruct(query.shape, jnp.bfloat16),
            jax.ShapeDtypeStruct(pages.shape, jnp.float32),
        ),
        in_specs=[pl.BlockSpec(memory_space=pltpu.SMEM), block, block, whole],
        out_specs=(block, whole),
        scratch_shapes=[
            pltpu.VMEM((chunks, HEAD_WIDTH, rows), jnp.bfloat16),
            pltpu.VMEM((chunks, rows, tokens), jnp.float32),
            pltpu.VMEM((chunks, rows, tokens), jnp.float32),
            pltpu.VMEM((chunks, rows, tokens), jnp.bfloat16),
        ],
        compiler_params=pltpu.CompilerParams(vmem_limit_bytes=32 * 2**20),
    )(lengths, query, upstream, pages)


def scatter_kernel(share, pages, tables, grads, grad_key, grad_value,
                   x_out, x_in, z_out, z_in, total, packed, stage, recv,
                   x_send, x_recv, z_send, z_recv, back_send, back_recv):
    own, head, own_x, own_z, rings = place()
    x_count = lax.axis_size("resp") // rings
    target, origin = spread_peers(own_x, own_z, head, rings, x_count)
    right, left, buddy = ring_peers(own_x, own_z, rings)
    messages = x_count * rings

    barrier = pltpu.get_barrier_semaphore()

    def greet(i, carry):
        x, h, z = target(i)
        pl.semaphore_signal(barrier, inc=1, device_id=(x * rings + z, h), device_id_type=MESH)
        return carry

    lax.fori_loop(0, messages, greet, 0)
    for peer in (right, left, buddy):
        pl.semaphore_signal(barrier, inc=1, device_id=(peer, head), device_id_type=MESH)

    side = lax.rem(own_x, 2)
    same = side * rings
    other = (1 - side) * rings
    hops = {1: rings // 2, -1: rings // 2 - 1}
    peers = {1: right, -1: left}
    copies = []
    x_moving, z_moving = {}, {}
    order = []
    for d in range(rings // 2, 0, -1):
        order += [d, -d] if d < rings // 2 else [d]
    order.append(0)
    for n, d in enumerate(order):
        x_out[n] = grads[other + mod(own_z + d, rings), 0].astype(jnp.bfloat16)
    pl.semaphore_wait(barrier, messages + 3)

    def x_push(n):
        copy = pltpu.make_async_remote_copy(
            src_ref=x_out.at[n], dst_ref=x_in.at[n], send_sem=x_send.at[n], recv_sem=x_recv.at[n],
            device_id=(buddy, head), device_id_type=MESH,
        )
        copy.start()
        copies.append(copy)
        x_moving[n] = copy

    def z_push(way, step, item, value):
        n = (way == -1) * 3 * hops[1] + step * 3 + item
        z_out[n] = value.astype(jnp.bfloat16)
        copy = pltpu.make_async_remote_copy(
            src_ref=z_out.at[n], dst_ref=z_in.at[n], send_sem=z_send.at[n], recv_sem=z_recv.at[n],
            device_id=(peers[way], head), device_id_type=MESH,
        )
        copy.start()
        copies.append(copy)
        z_moving[way, step, item] = (copy, n)

    def z_arrived(way, step, item):
        copy, n = z_moving[way, step, item]
        copy.wait_recv()
        return z_in[n].astype(jnp.float32)

    def own_term(item, d):
        spot = mod(own_z + d, rings)
        if item == 0:
            n = order.index(d)
            x_moving[n].wait_recv()
            return grads[same + spot, 0] + x_in[n].astype(jnp.float32)
        return grads[(same if item == 1 else other) + spot, 1]

    for n in range(rings):
        x_push(n)
    for step in range(rings // 2):
        for item in (1, 2, 0):
            for way in (1, -1):
                if step >= hops[way]:
                    continue
                d = way * (hops[way] - step)
                value = own_term(item, d)
                if step > 0:
                    value = value + z_arrived(way, step - 1, item)
                z_push(way, step, item, value)

    def finish(item):
        value = own_term(item, 0)
        for way in (1, -1):
            if hops[way]:
                value = value + z_arrived(way, hops[way] - 1, item)
        return value

    x_out[rings] = finish(2).astype(jnp.bfloat16)
    x_push(rings)
    total[0] = finish(0)
    value_total = finish(1)
    x_moving[rings].wait_recv()
    total[1] = value_total + x_in[rings].astype(jnp.float32)

    for n in range(rings):
        packed[n, :ROWS, :] = total[0, n * ROWS:(n + 1) * ROWS, :].astype(jnp.bfloat16)
        packed[n, ROWS:, :] = total[1, n * ROWS:(n + 1) * ROWS, :].astype(jnp.bfloat16)
    owners = prompt_owners(tables, own_x // 2, share, pages)
    for device in range(x_count * rings):
        rank = jnp.int32(0)
        for n, owner in enumerate(owners):
            rank = jnp.where(owner == device, n, rank)
        stage[device] = packed[rank]

    def send(i, carry):
        x, k, z = origin(i)
        pltpu.make_async_remote_copy(
            src_ref=stage.at[x * rings + z], dst_ref=recv.at[own_x, head],
            send_sem=back_send, recv_sem=back_recv,
            device_id=(x * rings + z, k), device_id_type=MESH,
        ).start()
        return carry

    lax.fori_loop(0, messages, send, 0)
    picked = []
    for prompt in range(x_count // 2):
        picked += local_slots(tables, prompt, own, share, pages)
    pltpu.make_async_copy(recv, recv, back_recv).wait()
    for page in range(PAGES_DEV):
        takes = [(slot == page).astype(jnp.float32) for slot in picked]
        for h in range(rings):
            columns = slice(h * HEAD_WIDTH, (h + 1) * HEAD_WIDTH)
            value = jnp.zeros((2 * ROWS, HEAD_WIDTH), jnp.float32)
            for n, take in enumerate(takes):
                value = value + recv[n, h].astype(jnp.float32) * take
            grad_key[page, :, columns] = value[:ROWS]
            grad_value[page, :, columns] = value[ROWS:]
    for copy in copies:
        copy.wait_send()
    pltpu.make_async_copy(stage, stage, back_send).wait()


def scattered(tables, grads, share, pages):
    rings = lax.axis_size("kvh")
    devices = lax.axis_size("resp")
    x_count = devices // rings
    rows = rings * ROWS
    z_copies = 3 * (rings - 1)
    block = pltpu.VMEM((rows, HEAD_WIDTH), jnp.bfloat16)
    out = jax.ShapeDtypeStruct((PAGES_DEV, ROWS, rings * HEAD_WIDTH), jnp.float32)
    return pl.pallas_call(
        functools.partial(scatter_kernel, share, pages),
        out_shape=(out, out),
        in_specs=[pl.BlockSpec(memory_space=pltpu.SMEM), pl.BlockSpec(memory_space=pltpu.VMEM)],
        out_specs=(pl.BlockSpec(memory_space=pltpu.VMEM),) * 2,
        scratch_shapes=[
            pltpu.VMEM((rings + 1, rows, HEAD_WIDTH), jnp.bfloat16),
            pltpu.VMEM((rings + 1, rows, HEAD_WIDTH), jnp.bfloat16),
            pltpu.VMEM((z_copies, rows, HEAD_WIDTH), jnp.bfloat16),
            pltpu.VMEM((z_copies, rows, HEAD_WIDTH), jnp.bfloat16),
            pltpu.VMEM((2, rows, HEAD_WIDTH), jnp.float32),
            pltpu.VMEM((rings, 2 * ROWS, HEAD_WIDTH), jnp.bfloat16),
            pltpu.VMEM((devices, 2 * ROWS, HEAD_WIDTH), jnp.bfloat16),
            pltpu.VMEM((x_count, rings, 2 * ROWS, HEAD_WIDTH), jnp.bfloat16),
            pltpu.SemaphoreType.DMA((rings + 1,)),
            pltpu.SemaphoreType.DMA((rings + 1,)),
            pltpu.SemaphoreType.DMA((z_copies,)),
            pltpu.SemaphoreType.DMA((z_copies,)),
            pltpu.SemaphoreType.DMA,
            pltpu.SemaphoreType.DMA,
        ],
        compiler_params=pltpu.CompilerParams(
            collective_id=1, has_side_effects=True, vmem_limit_bytes=24 * 2**20
        ),
    )(tables, grads)


def shards(query, output_gradient, prompt_key_pool, prompt_value_pool, block_tables, lengths):
    share = block_tables.shape[0] // (lax.axis_size("resp") // lax.axis_size("kvh") // 2)
    pages = block_tables.shape[1]
    held = gathered(block_tables, prompt_key_pool, prompt_value_pool, share, pages)
    grad_query, grads = attention_gradients(lengths, query[0], output_gradient[0], held)
    grad_key, grad_value = scattered(block_tables, grads, share, pages)
    return grad_query[None], grad_key, grad_value


def solution(mesh):
    placed = (
        P("resp", None, "kvh"),
        P("resp", None, "kvh"),
        P("resp", "kvh", None),
        P("resp", "kvh", None),
        P(),
        P("resp"),
    )
    return jax.shard_map(
        shards,
        mesh=mesh,
        in_specs=placed,
        out_specs=(P("resp", None, "kvh"), P("resp", "kvh", None), P("resp", "kvh", None)),
        check_vma=False,
    )
```

time: 715 us -> 141 us (0.20)
  waiting for transfers between devices: 587 us -> 0 us
  Pallas kernels: 0 us -> 134 us
  matrix products: 26.8 us -> 0 us
  local copies, waits for them, and re-layouts: 32.2 us -> 6.07 us
  blocking collectives: 19.7 us -> 0 us
  starting transfers between devices: 18 us -> 0 us
  other arithmetic: 16.2 us -> 0 us
  between operations: 14.6 us -> 1.31 us
    reduce_scatter x2 -> x0, waiting for transfers between devices: 438 us -> none  [the longest x1 221 us: shards(): lax.psum_scatter(full_values, 'resp', scatter_dimension=0, tiled=True)]
    all_gather x2 -> x0, waiting for transfers between devices: 144 us -> none  [the longest x1 79.4 us: shards(): lax.all_gather(head_values, 'resp', axis=0, tiled=True)]
    pallas_call x0 -> x3, Pallas kernels: none -> 134 us  [the longest x1 58.7 us: attention_gradients(): pl.pallas_call(functools.partial(attention_kernel, rows), grid=(groups,),...]
    dot_general x20 -> x0, matrix products: 26.8 us -> none  [the longest x4 7.64 us: one_block(): lax.dot_general(attention_b, upstream_block, contract_rows, preferred_ele...]
    all_to_all x2 -> x0, blocking collectives: 19.7 us -> none  [the longest x1 11.2 us: shards(): lax.all_to_all(prompt_key_pool, 'kvh', split_axis=2, concat_axis=1, tiled...]
    all_to_all x2 -> x0, starting transfers between devices: 17.6 us -> none  [the longest x1 8.83 us: shards(): lax.all_to_all(summed_keys, 'kvh', split_axis=1, concat_axis=2, tiled=True)]
    broadcast_in_dim x4 -> x0, local copies, waits for them, and re-layouts: 8.77 us -> none  [the longest x2 8.54 us: shards(): jnp.zeros((resp_count * pages_dev, page_tok, columns), jnp.float32)]
  transfers between devices with their start and end apart: 6 -> 0, of which waited for: 5 -> 0; matrix products, arithmetic and copies ran while one was open for 3% -> 0% of each run, Pallas kernels for 0% -> 0%
where the time goes in v1:
time: 141 us
  Pallas kernels  134 us (95%)
  local copies, waits for them, and re-layouts  6.07 us (4%)
    pallas_call x1, Pallas kernels, attention_gradients(): pl.pallas_call(functools.partial(attention_kernel, rows), grid=(groups,),...  58.7 us
    pallas_call x1, Pallas kernels, scattered(): pl.pallas_call(functools.partial(scatter_kernel, share, pages), out_shape...  37.8 us
    pallas_call x1, Pallas kernels, gathered(): pl.pallas_call(functools.partial(gather_kernel, share, pages), out_shape=...  37.3 us
    unnamed x11, local copies, waits for them, and re-layouts  6.07 us

profile of v1, /device:TPU:1, one launch (start us, length us, event | category | flops | bytes accessed | tf_op | source)
XLA Modules:
  0.0 141.1 jit_solution(10175838626663139711)
XLA Ops:
  1.3 0.8 copy.9.tables
  2.0 0.0 copy-start.2
  2.1 0.9 copy-done.2
  3.0 0.0 copy-start.3
  3.0 0.9 copy-done.3
  3.9 37.3 %shard_map.85.pages = bf16[16,2,128,128]{3,2,1,0:T(8,128)(2,1)S(1)} custom-call(s32[32,16]{1,0:T(8,128)S(1)} %copy.9.tables, bf16[4,16,1024]{2,1,0:T(8,128)(2,1)S(1)} %copy-done.2, bf16[4,16,1024]{2,1,0:T(8,128)(2,1)S(1)} %copy-done.3), custom_call_target="tpu_custom_call" | custom-call | tf_op jit(solution)/shard_map/pallas_call | solution.py:192
  41.1 0.0 copy-start
  41.1 1.0 copy-done
  42.2 0.0 copy-start.1
  42.2 1.0 copy-done.1
  43.2 58.7 %shard_map.86 = (bf16[256,1024]{1,0:T(8,128)(2,1)}, f32[16,2,128,128]{3,2,1,0:T(8,128)S(1)}) custom-call(s32[1]{0:T(128)S(6)} %copy.13.lengths, bf16[256,1024]{1,0:T(8,128)(2,1)S(1)} %bitcast.3, bf16[256,1024]{1,0:T(8,128)(2,1)S(1)} %bitcast.4, bf16[16,2,128,128]{3,2,1,0:T(8,128)(2,1)S(1)} %shard_map.85.pages), custom_call_target="tpu_custom_call" | custom-call | tf_op jit(solution)/shard_map/pallas_call | solution.py:277
  101.9 37.8 %shard_map.87 = (f32[4,16,1024]{2,1,0:T(8,128)S(1)}, f32[4,16,1024]{2,1,0:T(8,128)S(1)}) custom-call(s32[32,16]{1,0:T(8,128)S(1)} %copy.9.tables, f32[16,2,128,128]{3,2,1,0:T(8,128)S(1)} %get-tuple-element.8.grads), custom_call_target="tpu_custom_call" | custom-call | tf_op jit(solution)/shard_map/pallas_call | solution.py:437
  139.7 0.7 copy.14
  140.4 0.7 copy.15
Async XLA Ops:
  2.0 0.9 copy-start.2
  3.0 0.9 copy-start.3
  41.1 1.0 copy-start
  42.2 1.0 copy-start.1

commit v2 on v1

v2 whole, which is shorter than its diff:
```python
import functools

import jax
import jax.numpy as jnp
from jax import lax
from jax.experimental import pallas as pl
from jax.experimental.pallas import tpu as pltpu
from jax.sharding import PartitionSpec as P

QUERY_HEADS = 64
KEY_VALUE_HEADS = 8
HEAD_WIDTH = 128
PAGES_DEV = 4
SLOTS = 2
ROWS = 16
MESH = pl.DeviceIdType.MESH
LOG2E = 1.4426950408889634
STEP_ROWS = 512


def place():
    rings = lax.axis_size("kvh")
    own = lax.axis_index("resp")
    head = lax.axis_index("kvh")
    return own, head, own // rings, lax.rem(own, rings), rings


def mod(value, size):
    return lax.rem(value + 2 * size, size)


def local_slots(tables, prompt, own, share, pages):
    first, second, count = jnp.int32(-1), jnp.int32(-1), jnp.int32(0)
    for j in range(pages):
        page = tables[prompt * share, j]
        hit = (page // PAGES_DEV) == own
        local = lax.rem(page, PAGES_DEV)
        first = jnp.where(hit & (count == 0), local, first)
        second = jnp.where(hit & (count == 1), local, second)
        count = count + hit.astype(jnp.int32)
    return first, second


def prompt_owners(tables, prompt, share, pages):
    held = [tables[prompt * share, j] // PAGES_DEV for j in range(pages)]
    ranks = []
    for j in range(pages):
        below = jnp.int32(0)
        for i in range(pages):
            if i != j:
                below = below + (held[i] < held[j]).astype(jnp.int32)
        ranks.append(below // SLOTS)
    owners = []
    for n in range(pages // SLOTS):
        owner = jnp.int32(0)
        for j in range(pages):
            owner = jnp.where(ranks[j] == n, held[j], owner)
        owners.append(owner)
    return owners


def spread_peers(own_x, own_z, head, rings, x_count):
    def target(i):
        dx, dh = i // rings, lax.rem(i, rings)
        x = lax.rem(own_x + dx, x_count)
        h = lax.rem(head + dh, rings)
        z = mod(own_z - dh + 1, rings)
        return x, h, z

    def origin(i):
        dx, dk = i // rings, lax.rem(i, rings)
        x = lax.rem(own_x + dx, x_count)
        k = lax.rem(head + dk, rings)
        z = mod(own_z - dk - 1, rings)
        return x, k, z

    return target, origin


def ring_peers(own_x, own_z, rings):
    right = own_x * rings + lax.rem(own_z + 1, rings)
    left = own_x * rings + mod(own_z - 1, rings)
    buddy = (own_x + 1 - 2 * lax.rem(own_x, 2)) * rings + own_z
    return right, left, buddy


def attention_phase(length, query, upstream, pages, keys_t, work, soft, slopes, query_s, upstream_s, grad_query):
    tokens, width = query.shape
    groups = width // HEAD_WIDTH
    chunks, rows = pages.shape[1], pages.shape[2]
    count = chunks * rows
    step = min(STEP_ROWS, count)
    steps = count // step
    scale = HEAD_WIDTH ** -0.5
    pairs = soft.shape[0]
    pair_rows = soft.shape[1]
    for c in range(chunks):
        keys_t[:, c * rows:(c + 1) * rows] = pages[0, c].T

    def columns(g):
        return pl.ds(g * HEAD_WIDTH, HEAD_WIDTH)

    def lanes(g):
        return pl.ds(g * tokens, tokens)

    def span(n):
        return pl.ds(n * step, step)

    def block(n):
        return pl.ds(n * step // pair_rows, step // pair_rows)

    def held(part, n):
        return pages[part, n * step // rows:(n + 1) * step // rows].reshape(step, HEAD_WIDTH)

    def products(g, n, query_t, upstream_t, top):
        score, slope = work[g % 2]
        part = jnp.dot(held(0, n), query_t, preferred_element_type=jnp.float32) * (scale * LOG2E)
        score[span(n)] = part
        slope[span(n)] = jnp.dot(held(1, n), upstream_t, preferred_element_type=jnp.float32)
        return jnp.maximum(top, jnp.max(part.reshape(-1, 8, tokens), axis=0))

    lowest = jnp.full((8, tokens), -jnp.inf, jnp.float32)
    zero = jnp.zeros((8, tokens), jnp.float32)
    live = lax.broadcasted_iota(jnp.int32, (1, tokens), 1) < length
    query_t, upstream_t = query[:, columns(0)].T, upstream[:, columns(0)].T
    top = lowest
    for n in range(steps):
        top = products(0, n, query_t, upstream_t, top)
    before = None
    for g in range(groups + 1):
        if g < groups:
            score, slope = work[g % 2]
            peak = jnp.max(top, axis=0, keepdims=True)
            total, delta, top = zero, zero, lowest
            if g + 1 < groups:
                next_query, next_upstream = query[:, columns(g + 1)].T, upstream[:, columns(g + 1)].T
            for n in range(steps):
                if g + 1 < groups:
                    top = products(g + 1, n, next_query, next_upstream, top)
                part = jnp.exp2(score[span(n)] - peak)
                score[span(n)] = part
                soft[block(n), :, lanes(g)] = part.astype(jnp.bfloat16).reshape(-1, pair_rows, tokens)
                total = total + jnp.sum(part.reshape(-1, 8, tokens), axis=0)
                delta = delta + jnp.sum((part * slope[span(n)]).reshape(-1, 8, tokens), axis=0)
            inverse = 1.0 / jnp.sum(total, axis=0, keepdims=True)
            delta = jnp.sum(delta, axis=0, keepdims=True) * inverse
            inverse = jnp.where(live, inverse, 0.0)
            query_s[lanes(g)] = (query_t.astype(jnp.float32) * (inverse * scale)).T.astype(jnp.bfloat16)
            upstream_s[lanes(g)] = (upstream_t.astype(jnp.float32) * inverse).T.astype(jnp.bfloat16)
        if before is not None:
            last, factor = before
            spread_slopes = slopes[:, :, lanes(last)].reshape(count, tokens)
            result = jnp.dot(keys_t[...], spread_slopes, preferred_element_type=jnp.float32)
        if g < groups:
            for n in range(steps):
                part = (score[span(n)] * (slope[span(n)] - delta)).astype(jnp.bfloat16)
                slopes[block(n), :, lanes(g)] = part.reshape(-1, pair_rows, tokens)
        if before is not None:
            grad_query[:, columns(last)] = (result * factor).T.astype(jnp.bfloat16)
        if g < groups:
            before = (g, inverse * scale)
            if g + 1 < groups:
                query_t, upstream_t = next_query, next_upstream


def page_gradients(pair, tokens, soft, slopes, query_s, upstream_s, grads):
    groups = query_s.shape[0] // tokens
    for part, (left, right) in enumerate(((slopes, query_s), (soft, upstream_s))):
        value = 0.0
        for g in range(groups):
            lanes = pl.ds(g * tokens, tokens)
            value = value + jnp.dot(left[pair, :, lanes], right[lanes], preferred_element_type=jnp.float32)
        grads[pair, part] = value.reshape(SLOTS, -1, HEAD_WIDTH)


def whole_kernel(share, page_count, tables, lengths, query_hbm, upstream_hbm, key_pool, value_pool,
                 grad_query_hbm, grad_key, grad_value,
                 query, upstream, grad_query, pages, keys_t, score_a, slope_a, score_b, slope_b, soft, slopes,
                 query_s, upstream_s, grads, stage, recv, x_out, x_in, z_out, z_in, total, packed, back_stage, back,
                 copy_sem, spread_send, spread_recv, send_sem, recv_sem, x_send, x_recv, z_send, z_recv,
                 back_send, back_recv):
    own, head, own_x, own_z, rings = place()
    x_count = lax.axis_size("resp") // rings
    target, origin = spread_peers(own_x, own_z, head, rings, x_count)
    right, left, buddy = ring_peers(own_x, own_z, rings)
    messages = x_count * rings
    tokens = query.shape[0]
    side = lax.rem(own_x, 2)
    hops = {1: rings // 2, -1: rings // 2 - 1}
    peers = {1: right, -1: left}

    barrier = pltpu.get_barrier_semaphore()

    def greet(i, carry):
        x, h, z = target(i)
        pl.semaphore_signal(barrier, inc=1, device_id=(x * rings + z, h), device_id_type=MESH)
        x, k, z = origin(i)
        pl.semaphore_signal(barrier, inc=1, device_id=(x * rings + z, k), device_id_type=MESH)
        return carry

    lax.fori_loop(0, messages, greet, 0)
    for peer in (right, left, buddy):
        pl.semaphore_signal(barrier, inc=1, device_id=(peer, head), device_id_type=MESH)

    load_query = pltpu.make_async_copy(query_hbm, query, copy_sem.at[0])
    load_upstream = pltpu.make_async_copy(upstream_hbm, upstream, copy_sem.at[1])
    load_query.start()
    load_upstream.start()
    picked = []
    for prompt in range(x_count // 2):
        picked += local_slots(tables, prompt, own, share, page_count)
    for n, slot in enumerate(picked):
        page = jnp.maximum(slot, 0)
        for h in range(rings):
            columns = slice(h * HEAD_WIDTH, (h + 1) * HEAD_WIDTH)
            stage[n, h, :ROWS, :] = key_pool[page, :, columns]
            stage[n, h, ROWS:, :] = value_pool[page, :, columns]
    pl.semaphore_wait(barrier, 2 * messages + 3)

    def send(i, carry):
        x, h, z = target(i)
        pltpu.make_async_remote_copy(
            src_ref=stage.at[x, h], dst_ref=recv.at[own], send_sem=spread_send, recv_sem=spread_recv,
            device_id=(x * rings + z, h), device_id_type=MESH,
        ).start()
        return carry

    lax.fori_loop(0, messages, send, 0)
    owners = prompt_owners(tables, own_x // 2, share, page_count)
    pltpu.make_async_copy(recv, recv, spread_recv).wait()

    mine = 2 * own_z + side
    for n, owner in enumerate(owners):
        piece = recv[owner]
        pages[0, mine, n * ROWS:(n + 1) * ROWS, :] = piece[:ROWS]
        pages[1, mine, n * ROWS:(n + 1) * ROWS, :] = piece[ROWS:]

    copies = []
    moving = {}

    def push(name, chunk, part, peer):
        slot = len(moving)
        copy = pltpu.make_async_remote_copy(
            src_ref=pages.at[part, chunk], dst_ref=pages.at[part, chunk],
            send_sem=send_sem.at[slot], recv_sem=recv_sem.at[slot],
            device_id=(peer, head), device_id_type=MESH,
        )
        copy.start()
        copies.append(copy)
        moving[name] = copy

    push(("x", 1), mine, 1, buddy)
    for way in (1, -1):
        for part in (0, 1):
            push(("z", way, 0, part, 0), mine, part, peers[way])
    push(("x", 0, 0), mine, 0, buddy)
    moving["x", 1].wait_recv()
    for way in (1, -1):
        push(("z", way, 0, 1, 1), 2 * own_z + 1 - side, 1, peers[way])
    for step in range(1, rings // 2 + 1):
        for part, flip in ((0, 0), (1, 0), (1, 1)):
            for way in (1, -1):
                if step > hops[way]:
                    continue
                moving["z", way, step - 1, part, flip].wait_recv()
                chunk = 2 * mod(own_z - way * step, rings) + (1 - side if flip else side)
                if step < hops[way]:
                    push(("z", way, step, part, flip), chunk, part, peers[way])
                if part == 0:
                    push(("x", 0, way * step), chunk, part, buddy)
    for name, copy in moving.items():
        if name[0] == "x" and name[1] == 0:
            copy.wait_recv()

    load_query.wait()
    load_upstream.wait()
    attention_phase(lengths[0], query, upstream, pages, keys_t, ((score_a, slope_a), (score_b, slope_b)),
                    soft, slopes, query_s, upstream_s, grad_query)
    store_query = pltpu.make_async_copy(grad_query, grad_query_hbm, copy_sem.at[0])
    store_query.start()

    order = []
    for step in range(rings // 2):
        order += [way * (hops[way] - step) for way in (1, -1) if step < hops[way]]
    order.append(0)
    x_moving, z_moving = {}, {}

    def x_push(n):
        copy = pltpu.make_async_remote_copy(
            src_ref=x_out.at[n], dst_ref=x_in.at[n], send_sem=x_send.at[n], recv_sem=x_recv.at[n],
            device_id=(buddy, head), device_id_type=MESH,
        )
        copy.start()
        copies.append(copy)
        x_moving[n] = copy

    def own_term(item, d):
        spot = mod(own_z + d, rings)
        if item == 0:
            n = order.index(d)
            x_moving[n].wait_recv()
            return grads[spot, 0, side] + x_in[n].astype(jnp.float32)
        return grads[spot, 1, side if item == 1 else 1 - side]

    def z_arrived(way, step, item):
        copy, n = z_moving[way, step, item]
        copy.wait_recv()
        return z_in[n].astype(jnp.float32)

    def z_push(item, d):
        way = 1 if d > 0 else -1
        step = hops[way] - abs(d)
        value = own_term(item, d)
        if step > 0:
            value = value + z_arrived(way, step - 1, item)
        n = (way == -1) * 3 * hops[1] + step * 3 + item
        z_out[n] = value.astype(jnp.bfloat16)
        copy = pltpu.make_async_remote_copy(
            src_ref=z_out.at[n], dst_ref=z_in.at[n], send_sem=z_send.at[n], recv_sem=z_recv.at[n],
            device_id=(peers[way], head), device_id_type=MESH,
        )
        copy.start()
        copies.append(copy)
        z_moving[way, step, item] = (copy, n)

    def finish(item):
        value = own_term(item, 0)
        for way in (1, -1):
            if hops[way]:
                value = value + z_arrived(way, hops[way] - 1, item)
        return value

    for n, d in enumerate(order):
        spot = mod(own_z + d, rings)
        page_gradients(spot, tokens, soft, slopes, query_s, upstream_s, grads)
        x_out[n] = grads[spot, 0, 1 - side].astype(jnp.bfloat16)
        x_push(n)
        if d != 0:
            z_push(1, d)
            z_push(2, d)
        if n > 0:
            z_push(0, order[n - 1])
    x_out[rings] = finish(2).astype(jnp.bfloat16)
    x_push(rings)
    total[0] = finish(0)
    value_total = finish(1)
    x_moving[rings].wait_recv()
    total[1] = value_total + x_in[rings].astype(jnp.float32)

    for n in range(rings):
        packed[n, :ROWS, :] = total[0, n * ROWS:(n + 1) * ROWS, :].astype(jnp.bfloat16)
        packed[n, ROWS:, :] = total[1, n * ROWS:(n + 1) * ROWS, :].astype(jnp.bfloat16)
    for device in range(x_count * rings):
        rank = jnp.int32(0)
        for n, owner in enumerate(owners):
            rank = jnp.where(owner == device, n, rank)
        back_stage[device] = packed[rank]

    def send_back(i, carry):
        x, k, z = origin(i)
        pltpu.make_async_remote_copy(
            src_ref=back_stage.at[x * rings + z], dst_ref=back.at[own_x, head],
            send_sem=back_send, recv_sem=back_recv,
            device_id=(x * rings + z, k), device_id_type=MESH,
        ).start()
        return carry

    lax.fori_loop(0, messages, send_back, 0)
    pltpu.make_async_copy(back, back, back_recv).wait()
    for page in range(PAGES_DEV):
        takes = [(slot == page).astype(jnp.float32) for slot in picked]
        for h in range(rings):
            columns = slice(h * HEAD_WIDTH, (h + 1) * HEAD_WIDTH)
            value = jnp.zeros((2 * ROWS, HEAD_WIDTH), jnp.float32)
            for n, take in enumerate(takes):
                value = value + back[n, h].astype(jnp.float32) * take
            grad_key[page, :, columns] = value[:ROWS]
            grad_value[page, :, columns] = value[ROWS:]
    for copy in copies:
        copy.wait_send()
    pltpu.make_async_copy(stage, stage, spread_send).wait()
    pltpu.make_async_copy(back_stage, back_stage, back_send).wait()
    store_query.wait()


def gradients(tables, lengths, query, upstream, key_pool, value_pool):
    rings = lax.axis_size("kvh")
    devices = lax.axis_size("resp")
    x_count = devices // rings
    share = 2 * rings
    page_count = tables.shape[1]
    tokens, width = query.shape
    rows = rings * ROWS
    chunks = SLOTS * rings
    count = chunks * rows
    query_rows = tokens * (width // HEAD_WIDTH)
    z_copies = 3 * (rings - 1)
    gathers = 1 + rings + z_copies
    out = jax.ShapeDtypeStruct((PAGES_DEV, ROWS, rings * HEAD_WIDTH), jnp.float32)
    bf16, f32 = jnp.bfloat16, jnp.float32
    vmem = pl.BlockSpec(memory_space=pltpu.VMEM)
    smem = pl.BlockSpec(memory_space=pltpu.SMEM)
    anywhere = pl.BlockSpec(memory_space=pl.ANY)
    dma = pltpu.SemaphoreType.DMA
    return pl.pallas_call(
        functools.partial(whole_kernel, share, page_count),
        out_shape=(jax.ShapeDtypeStruct(query.shape, bf16), out, out),
        in_specs=[smem, smem, anywhere, anywhere, vmem, vmem],
        out_specs=(anywhere, vmem, vmem),
        scratch_shapes=[
            pltpu.VMEM((tokens, width), bf16),
            pltpu.VMEM((tokens, width), bf16),
            pltpu.VMEM((tokens, width), bf16),
            pltpu.VMEM((2, chunks, rows, HEAD_WIDTH), bf16),
            pltpu.VMEM((HEAD_WIDTH, count), bf16),
            pltpu.VMEM((count, tokens), f32),
            pltpu.VMEM((count, tokens), f32),
            pltpu.VMEM((count, tokens), f32),
            pltpu.VMEM((count, tokens), f32),
            pltpu.VMEM((rings, 2 * rows, query_rows), bf16),
            pltpu.VMEM((rings, 2 * rows, query_rows), bf16),
            pltpu.VMEM((query_rows, HEAD_WIDTH), bf16),
            pltpu.VMEM((query_rows, HEAD_WIDTH), bf16),
            pltpu.VMEM((rings, 2, SLOTS, rows, HEAD_WIDTH), f32),
            pltpu.VMEM((x_count, rings, 2 * ROWS, HEAD_WIDTH), bf16),
            pltpu.VMEM((devices, 2 * ROWS, HEAD_WIDTH), bf16),
            pltpu.VMEM((rings + 1, rows, HEAD_WIDTH), bf16),
            pltpu.VMEM((rings + 1, rows, HEAD_WIDTH), bf16),
            pltpu.VMEM((z_copies, rows, HEAD_WIDTH), bf16),
            pltpu.VMEM((z_copies, rows, HEAD_WIDTH), bf16),
            pltpu.VMEM((2, rows, HEAD_WIDTH), f32),
            pltpu.VMEM((rings, 2 * ROWS, HEAD_WIDTH), bf16),
            pltpu.VMEM((devices, 2 * ROWS, HEAD_WIDTH), bf16),
            pltpu.VMEM((x_count, rings, 2 * ROWS, HEAD_WIDTH), bf16),
            dma((2,)),
            dma,
            dma,
            dma((gathers,)),
            dma((gathers,)),
            dma((rings + 1,)),
            dma((rings + 1,)),
            dma((z_copies,)),
            dma((z_copies,)),
            dma,
            dma,
        ],
        compiler_params=pltpu.CompilerParams(
            collective_id=0, has_side_effects=True, vmem_limit_bytes=48 * 2**20
        ),
    )(tables, lengths, query, upstream, key_pool, value_pool)


def shards(query, output_gradient, prompt_key_pool, prompt_value_pool, block_tables, lengths):
    grad_query, grad_key, grad_value = gradients(
        block_tables, lengths, query[0], output_gradient[0], prompt_key_pool, prompt_value_pool
    )
    return grad_query[None], grad_key, grad_value


def solution(mesh):
    placed = (
        P("resp", None, "kvh"),
        P("resp", None, "kvh"),
        P("resp", "kvh", None),
        P("resp", "kvh", None),
        P(),
        P("resp"),
    )
    return jax.shard_map(
        shards,
        mesh=mesh,
        in_specs=placed,
        out_specs=(P("resp", None, "kvh"), P("resp", "kvh", None), P("resp", "kvh", None)),
        check_vma=False,
    )
```

time: 141 us -> 95.6 us (0.68)
  Pallas kernels: 134 us -> 87.2 us
    pallas_call x3 -> x1, Pallas kernels: 134 us -> 87.2 us  [gradients(): pl.pallas_call(functools.partial(whole_kernel, share, page_count), out_sh...]
    unnamed x11 -> x12, local copies, waits for them, and re-layouts: 6.07 us -> 6.86 us
where the time goes in v2:
time: 95.6 us; the launch traced here: 95.3 us
  Pallas kernels  87.2 us (91%)
  local copies, waits for them, and re-layouts  6.86 us (7%)
  between operations  1.29 us (1%)
    pallas_call x1, Pallas kernels, gradients(): pl.pallas_call(functools.partial(whole_kernel, share, page_count), out_sh...  87.2 us
    unnamed x12, local copies, waits for them, and re-layouts  6.86 us

profile of v2, /device:TPU:1, one launch (start us, length us, event | category | flops | bytes accessed | tf_op | source)
XLA Modules:
  0.0 95.3 jit_solution(3228990151172179488)
XLA Ops:
  1.3 0.8 copy.9.tables
  2.0 0.0 copy-start
  2.1 1.0 %copy-done = bf16[1,256,1024]{2,1,0:T(8,128)(2,1)S(1)} copy-done((bf16[1,256,1024]{2,1,0:T(8,128)(2,1)S(1)}, bf16[1,256,1024]{2,1,0:T(8,128)(2,1)}, u32[]{:S(2)}) %copy-start) | copy-done | bytes 524312
  3.1 0.0 copy-start.1
  3.1 1.0 %copy-done.1 = bf16[1,256,1024]{2,1,0:T(8,128)(2,1)S(1)} copy-done((bf16[1,256,1024]{2,1,0:T(8,128)(2,1)S(1)}, bf16[1,256,1024]{2,1,0:T(8,128)(2,1)}, u32[]{:S(2)}) %copy-start.1) | copy-done | bytes 524312
  4.1 0.0 copy-start.2
  4.1 0.9 copy-done.2
  5.0 0.0 copy-start.3
  5.0 0.9 copy-done.3
  5.9 87.2 %shard_map.85 = (bf16[256,1024]{1,0:T(8,128)(2,1)S(1)}, f32[4,16,1024]{2,1,0:T(8,128)S(1)}, f32[4,16,1024]{2,1,0:T(8,128)S(1)}) custom-call(s32[32,16]{1,0:T(8,128)S(1)} %copy.9.tables, s32[1]{0:T(128)S(6)} %copy.13.lengths, bf16[256,1024]{1,0:T(8,128)(2,1)S(1)} %bitcast.3, bf16[256,1024]{1,0:T(8,128)(2,1)S(1)} %bitcast.4, ...), custom_call_target="tpu_custom_call" | custom-call | tf_op jit(solution)/shard_map/pallas_call | solution.py:405
  93.1 0.8 copy.14
  93.9 0.7 copy.15
  94.6 0.7 copy.16
Async XLA Ops:
  2.0 1.0 %copy-start = (bf16[1,256,1024]{2,1,0:T(8,128)(2,1)S(1)}, bf16[1,256,1024]{2,1,0:T(8,128)(2,1)}, u32[]{:S(2)}) copy-start(bf16[1,256,1024]{2,1,0:T(8,128)(2,1)} %param.6) | copy-start | bytes 1572868
  3.1 1.0 %copy-start.1 = (bf16[1,256,1024]{2,1,0:T(8,128)(2,1)S(1)}, bf16[1,256,1024]{2,1,0:T(8,128)(2,1)}, u32[]{:S(2)}) copy-start(bf16[1,256,1024]{2,1,0:T(8,128)(2,1)} %param.7) | copy-start | bytes 1572868
  4.1 0.9 copy-start.2
  5.0 0.9 copy-start.3

commit v3 on v2

v3 whole, which is shorter than its diff:
```python
import functools

import jax
import jax.numpy as jnp
from jax import lax
from jax.experimental import pallas as pl
from jax.experimental.pallas import tpu as pltpu
from jax.sharding import PartitionSpec as P

QUERY_HEADS = 64
KEY_VALUE_HEADS = 8
HEAD_WIDTH = 128
PAGES_DEV = 4
SLOTS = 2
ROWS = 16
MESH = pl.DeviceIdType.MESH
LOG2E = 1.4426950408889634
STEP_ROWS = 512


def place():
    rings = lax.axis_size("kvh")
    own = lax.axis_index("resp")
    head = lax.axis_index("kvh")
    return own, head, own // rings, lax.rem(own, rings), rings


def mod(value, size):
    return lax.rem(value + 2 * size, size)


def local_slots(tables, prompt, own, share, pages):
    first, second, count = jnp.int32(-1), jnp.int32(-1), jnp.int32(0)
    for j in range(pages):
        page = tables[prompt * share, j]
        hit = (page // PAGES_DEV) == own
        local = lax.rem(page, PAGES_DEV)
        first = jnp.where(hit & (count == 0), local, first)
        second = jnp.where(hit & (count == 1), local, second)
        count = count + hit.astype(jnp.int32)
    return first, second


def prompt_owners(tables, prompt, share, pages):
    held = [tables[prompt * share, j] // PAGES_DEV for j in range(pages)]
    ranks = []
    for j in range(pages):
        below = jnp.int32(0)
        for i in range(pages):
            if i != j:
                below = below + (held[i] < held[j]).astype(jnp.int32)
        ranks.append(below // SLOTS)
    owners = []
    for n in range(pages // SLOTS):
        owner = jnp.int32(0)
        for j in range(pages):
            owner = jnp.where(ranks[j] == n, held[j], owner)
        owners.append(owner)
    return owners


def spread_peers(own_x, own_z, head, rings, x_count):
    def target(i):
        dx, dh = i // rings, lax.rem(i, rings)
        x = lax.rem(own_x + dx, x_count)
        h = lax.rem(head + dh, rings)
        z = mod(own_z - dh + 1, rings)
        return x, h, z

    def origin(i):
        dx, dk = i // rings, lax.rem(i, rings)
        x = lax.rem(own_x + dx, x_count)
        k = lax.rem(head + dk, rings)
        z = mod(own_z - dk - 1, rings)
        return x, k, z

    return target, origin


def attention_phase(length, query, upstream, pages, keys_t, work, turned, soft, slopes, query_s, upstream_s, grad_query):
    tokens, width = query.shape
    groups = width // HEAD_WIDTH
    chunks, rows = pages.shape[1], pages.shape[2]
    count = chunks * rows
    step = min(STEP_ROWS, count)
    steps = count // step
    scale = HEAD_WIDTH ** -0.5
    pair_rows = soft.shape[1]
    for c in range(chunks):
        keys_t[:, c * rows:(c + 1) * rows] = pages[0, c].T

    def columns(g):
        return pl.ds(pl.multiple_of(g * HEAD_WIDTH, HEAD_WIDTH), HEAD_WIDTH)

    def lanes(g):
        return pl.ds(pl.multiple_of(g * tokens, tokens), tokens)

    def span(n):
        return pl.ds(n * step, step)

    def block(n):
        return pl.ds(n * step // pair_rows, step // pair_rows)

    def held(part, n):
        return pages[part, n * step // rows:(n + 1) * step // rows].reshape(step, HEAD_WIDTH)

    lowest = jnp.full((8, tokens), -jnp.inf, jnp.float32)
    zero = jnp.zeros((8, tokens), jnp.float32)
    live = lax.broadcasted_iota(jnp.int32, (1, tokens), 1) < length

    def turn(g, side):
        query_t, upstream_t = turned[side]
        query_t[...] = query[:, columns(g)].T
        upstream_t[...] = upstream[:, columns(g)].T

    def products(side, n, top):
        query_t, upstream_t = turned[side]
        score, slope = work[side]
        part = jnp.dot(held(0, n), query_t[...], preferred_element_type=jnp.float32) * (scale * LOG2E)
        score[span(n)] = part
        slope[span(n)] = jnp.dot(held(1, n), upstream_t[...], preferred_element_type=jnp.float32)
        return jnp.maximum(top, jnp.max(part.reshape(-1, 8, tokens), axis=0))

    def query_products(g):
        block_slopes = slopes[:, :, lanes(g)].reshape(count, tokens)
        return jnp.dot(keys_t[...], block_slopes, preferred_element_type=jnp.float32)

    def one_group(g, side, top, before, factor, after):
        score, slope = work[side]
        peak = jnp.max(top, axis=0, keepdims=True)
        total, delta, top = zero, zero, lowest
        turn(after, 1 - side)
        for n in range(steps):
            top = products(1 - side, n, top)
            part = jnp.exp2(score[span(n)] - peak)
            score[span(n)] = part
            soft[block(n), :, lanes(g)] = part.astype(jnp.bfloat16).reshape(-1, pair_rows, tokens)
            total = total + jnp.sum(part.reshape(-1, 8, tokens), axis=0)
            delta = delta + jnp.sum((part * slope[span(n)]).reshape(-1, 8, tokens), axis=0)
        inverse = 1.0 / jnp.sum(total, axis=0, keepdims=True)
        delta = jnp.sum(delta, axis=0, keepdims=True) * inverse
        inverse = jnp.where(live, inverse, 0.0)
        query_t, upstream_t = turned[side]
        query_s[lanes(g)] = (query_t[...].astype(jnp.float32) * (inverse * scale)).T.astype(jnp.bfloat16)
        upstream_s[lanes(g)] = (upstream_t[...].astype(jnp.float32) * inverse).T.astype(jnp.bfloat16)
        result = query_products(before)
        for n in range(steps):
            part = (score[span(n)] * (slope[span(n)] - delta)).astype(jnp.bfloat16)
            slopes[block(n), :, lanes(g)] = part.reshape(-1, pair_rows, tokens)
        grad_query[:, columns(before)] = (result * factor).T.astype(jnp.bfloat16)
        return top, inverse * scale

    final = groups - 1
    slopes[:, :, final * tokens:] = jnp.zeros((slopes.shape[0], pair_rows, tokens), jnp.bfloat16)
    turn(0, 0)
    top = lowest
    for n in range(steps):
        top = products(0, n, top)

    def two_groups(i, carry):
        top, factor = carry
        g = 2 * i
        top, factor = one_group(g, 0, top, lax.rem(g + final, groups), factor, g + 1)
        return one_group(g + 1, 1, top, g, factor, lax.rem(g + 2, groups))

    top, factor = lax.fori_loop(0, groups // 2, two_groups, (top, jnp.zeros((1, tokens), jnp.float32)))
    grad_query[:, final * HEAD_WIDTH:] = (query_products(final) * factor).T.astype(jnp.bfloat16)


def page_gradients(pair, tokens, soft, slopes, query_s, upstream_s, grads):
    groups = query_s.shape[0] // tokens
    for part, (left, right) in enumerate(((slopes, query_s), (soft, upstream_s))):
        value = 0.0
        for g in range(groups):
            lanes = pl.ds(g * tokens, tokens)
            value = value + jnp.dot(left[pair, :, lanes], right[lanes], preferred_element_type=jnp.float32)
        grads[pair, part] = value.reshape(SLOTS, -1, HEAD_WIDTH)


def whole_kernel(share, page_count, tables, lengths, query_hbm, upstream_hbm, key_hbm, value_hbm,
                 grad_query_hbm, grad_key, grad_value,
                 key_pool, value_pool, ranks, query, upstream, grad_query, pages, keys_t, query_a, upstream_a,
                 query_b, upstream_b, score_a, slope_a, score_b, slope_b, soft, slopes,
                 query_s, upstream_s, grads, stage, recv, x_out, x_in, z_out, z_in, total, packed, back_stage, back,
                 copy_sem, spread_send, spread_recv, send_sem, recv_sem, x_send, x_recv, z_send, z_recv,
                 back_send, back_recv):
    own, head, own_x, own_z, rings = place()
    x_count = lax.axis_size("resp") // rings
    target, origin = spread_peers(own_x, own_z, head, rings, x_count)
    buddy = (own_x + 1 - 2 * lax.rem(own_x, 2)) * rings + own_z

    def ring(d):
        return own_x * rings + mod(own_z + d, rings)

    neighbours = [buddy] + [ring(d) for d in ((1, -1, 2, -2) if rings > 4 else (1, -1, 2))]
    messages = x_count * rings
    tokens = query.shape[0]
    side = lax.rem(own_x, 2)
    half = rings // 2
    loads = [
        pltpu.make_async_copy(source, place, copy_sem.at[n])
        for n, (source, place) in enumerate(
            ((key_hbm, key_pool), (value_hbm, value_pool), (query_hbm, query), (upstream_hbm, upstream))
        )
    ]
    for load in loads:
        load.start()
    barrier = pltpu.get_barrier_semaphore()

    def greet(i, carry):
        x, h, z = target(i)
        pl.semaphore_signal(barrier, inc=1, device_id=(x * rings + z, h), device_id_type=MESH)
        x, k, z = origin(i)
        pl.semaphore_signal(barrier, inc=1, device_id=(x * rings + z, k), device_id_type=MESH)
        return carry

    lax.fori_loop(0, messages, greet, 0)
    for peer in neighbours:
        pl.semaphore_signal(barrier, inc=1, device_id=(peer, head), device_id_type=MESH)

    picked = []
    for prompt in range(x_count // 2):
        picked += local_slots(tables, prompt, own, share, page_count)
    loads[0].wait()
    loads[1].wait()
    for n, slot in enumerate(picked):
        page = jnp.maximum(slot, 0)
        for h in range(rings):
            columns = slice(h * HEAD_WIDTH, (h + 1) * HEAD_WIDTH)
            stage[n, h, :ROWS, :] = key_pool[page, :, columns]
            stage[n, h, ROWS:, :] = value_pool[page, :, columns]
    pl.semaphore_wait(barrier, 2 * messages + len(neighbours))

    def send(i, carry):
        x, h, z = target(i)
        pltpu.make_async_remote_copy(
            src_ref=stage.at[x, h], dst_ref=recv.at[own], send_sem=spread_send, recv_sem=spread_recv,
            device_id=(x * rings + z, h), device_id_type=MESH,
        ).start()
        return carry

    lax.fori_loop(0, messages, send, 0)
    owners = prompt_owners(tables, own_x // 2, share, page_count)
    for device in range(x_count * rings):
        rank = jnp.int32(0)
        for n, owner in enumerate(owners):
            rank = jnp.where(owner == device, n, rank)
        ranks[device] = rank
    pltpu.make_async_copy(recv, recv, spread_recv).wait()

    mine = 2 * own_z + side
    for n, owner in enumerate(owners):
        piece = recv[owner]
        pages[0, mine, n * ROWS:(n + 1) * ROWS, :] = piece[:ROWS]
        pages[1, mine, n * ROWS:(n + 1) * ROWS, :] = piece[ROWS:]

    copies = []
    moving = {}

    def push(name, chunk, part, peer):
        slot = len(moving)
        copy = pltpu.make_async_remote_copy(
            src_ref=pages.at[part, chunk], dst_ref=pages.at[part, chunk],
            send_sem=send_sem.at[slot], recv_sem=recv_sem.at[slot],
            device_id=(peer, head), device_id_type=MESH,
        )
        copy.start()
        copies.append(copy)
        moving[name] = copy

    def relay(d, part):
        way = 1 if d > 0 else -1
        chunk = 2 * mod(own_z - d, rings) + side
        push(("z", d + way, part), chunk, part, ring(way))
        if part == (0 if way > 0 else 1):
            push(("z", half, part), chunk, part, ring(2 * way))

    for part in (0, 1):
        push(("x", part, 0), mine, part, buddy)
    for d in ((2, -2, 1, -1) if half == 4 else (2, 1, -1)):
        for part in (0, 1):
            push(("z", d, part), mine, part, ring(d))
    for d in ((2, -2, 0, 3, -3, 4, 1, -1) if half == 4 else (0, 2, 1, -1)):
        for part in (0, 1):
            if d == 0:
                moving["x", part, 0].wait_recv()
                for near in (1, -1):
                    push(("w", near, part), 2 * own_z + 1 - side, part, ring(near))
                continue
            moving["z", d, part].wait_recv()
            if half == 4 and abs(d) == 2:
                relay(d, part)
            if abs(d) > 1:
                push(("x", part, d), 2 * mod(own_z - d, rings) + side, part, buddy)
    for name, copy in moving.items():
        if name[0] == "w" or name[0] == "x" and name[2] != 0:
            copy.wait_recv()

    loads[2].wait()
    loads[3].wait()
    attention_phase(lengths[0], query, upstream, pages, keys_t, ((score_a, slope_a), (score_b, slope_b)),
                    ((query_a, upstream_a), (query_b, upstream_b)), soft, slopes, query_s, upstream_s, grad_query)
    store_query = pltpu.make_async_copy(grad_query, grad_query_hbm, copy_sem.at[0])
    store_query.start()

    far = [4, 3, -3, 2, -2] if half == 4 else [2]
    x_moving, z_moving = {}, {}

    def x_push(n, d, added):
        for part in (0, 1):
            value = grads[mod(own_z + d, rings), part, 1 - side]
            for term in added:
                value = value + z_arrived(term, part)
            x_out[n, part] = value.astype(jnp.bfloat16)
        copy = pltpu.make_async_remote_copy(
            src_ref=x_out.at[n], dst_ref=x_in.at[n], send_sem=x_send.at[n], recv_sem=x_recv.at[n],
            device_id=(buddy, head), device_id_type=MESH,
        )
        copy.start()
        copies.append(copy)
        x_moving[n] = copy

    def z_arrived(name, part):
        copy, n = z_moving[name, part]
        copy.wait_recv()
        return z_in[n].astype(jnp.float32)

    def z_push(name, part, value, device):
        n = len(z_moving)
        z_out[n] = value.astype(jnp.bfloat16)
        copy = pltpu.make_async_remote_copy(
            src_ref=z_out.at[n], dst_ref=z_in.at[n], send_sem=z_send.at[n], recv_sem=z_recv.at[n],
            device_id=(device, head), device_id_type=MESH,
        )
        copy.start()
        copies.append(copy)
        z_moving[name, part] = (copy, n)

    def far_push(d):
        n = far.index(d)
        way = 1 if d > 0 else -1
        x_moving[n].wait_recv()
        for part in (0, 1):
            value = grads[mod(own_z + d, rings), part, side] + x_in[n, part].astype(jnp.float32)
            if half == 4 and abs(d) == 2:
                value = value + z_arrived(("far", 3 * way), part)
                if part == (0 if way > 0 else 1):
                    value = value + z_arrived(("far", 4), part)
            if abs(d) == 2:
                z_push(("far", d), part, value, ring(d))
            elif abs(d) == 3:
                z_push(("far", d), part, value, ring(way))
            else:
                z_push(("far", d), part, value, ring(2 if part == 0 else -2))

    def near_push(d):
        for flip in (0, 1):
            for part in (0, 1):
                value = grads[mod(own_z + d, rings), part, 1 - side if flip else side]
                z_push(("near", d, flip), part, value, ring(d))

    def compute(d):
        page_gradients(mod(own_z + d, rings), tokens, soft, slopes, query_s, upstream_s, grads)

    for n, d in enumerate(far):
        compute(d)
        x_push(n, d, ())
    early = [d for d in far if abs(d) > 2]
    late = [d for d in far if abs(d) == 2]
    for n, d in enumerate((1, -1, 0)):
        compute(d)
        if d != 0:
            near_push(d)
        if n < len(early):
            far_push(early[n])
    x_push(len(far), 0, (("near", 1, 1), ("near", -1, 1)))
    for d in late:
        far_push(d)
    for part in (0, 1):
        value = grads[own_z, part, side]
        for name in [("near", 1, 0), ("near", -1, 0)] + [("far", d) for d in late]:
            value = value + z_arrived(name, part)
        if part == 0:
            x_moving[len(far)].wait_recv()
        total[part] = value + x_in[len(far), part].astype(jnp.float32)

    for n in range(rings):
        packed[n, :ROWS, :] = total[0, n * ROWS:(n + 1) * ROWS, :].astype(jnp.bfloat16)
        packed[n, ROWS:, :] = total[1, n * ROWS:(n + 1) * ROWS, :].astype(jnp.bfloat16)
    for device in range(x_count * rings):
        back_stage[device] = packed[ranks[device]]

    def send_back(i, carry):
        x, k, z = origin(i)
        pltpu.make_async_remote_copy(
            src_ref=back_stage.at[x * rings + z], dst_ref=back.at[own_x, head],
            send_sem=back_send, recv_sem=back_recv,
            device_id=(x * rings + z, k), device_id_type=MESH,
        ).start()
        return carry

    lax.fori_loop(0, messages, send_back, 0)
    pltpu.make_async_copy(back, back, back_recv).wait()
    for page in range(PAGES_DEV):
        takes = [(slot == page).astype(jnp.float32) for slot in picked]
        for h in range(rings):
            columns = slice(h * HEAD_WIDTH, (h + 1) * HEAD_WIDTH)
            value = jnp.zeros((2 * ROWS, HEAD_WIDTH), jnp.float32)
            for n, take in enumerate(takes):
                value = value + back[n, h].astype(jnp.float32) * take
            grad_key[page, :, columns] = value[:ROWS]
            grad_value[page, :, columns] = value[ROWS:]
    for copy in copies:
        copy.wait_send()
    pltpu.make_async_copy(stage, stage, spread_send).wait()
    pltpu.make_async_copy(back_stage, back_stage, back_send).wait()
    store_query.wait()


def gradients(tables, lengths, query, upstream, key_pool, value_pool):
    rings = lax.axis_size("kvh")
    devices = lax.axis_size("resp")
    x_count = devices // rings
    share = 2 * rings
    page_count = tables.shape[1]
    tokens, width = query.shape
    rows = rings * ROWS
    chunks = SLOTS * rings
    count = chunks * rows
    query_rows = tokens * (width // HEAD_WIDTH)
    z_copies = 2 * rings + 2
    gathers = 4 * rings - 2
    out = jax.ShapeDtypeStruct((PAGES_DEV, ROWS, rings * HEAD_WIDTH), jnp.float32)
    bf16, f32 = jnp.bfloat16, jnp.float32
    vmem = pl.BlockSpec(memory_space=pltpu.VMEM)
    smem = pl.BlockSpec(memory_space=pltpu.SMEM)
    anywhere = pl.BlockSpec(memory_space=pl.ANY)
    dma = pltpu.SemaphoreType.DMA
    return pl.pallas_call(
        functools.partial(whole_kernel, share, page_count),
        out_shape=(jax.ShapeDtypeStruct(query.shape, bf16), out, out),
        in_specs=[smem, smem, anywhere, anywhere, anywhere, anywhere],
        out_specs=(anywhere, vmem, vmem),
        scratch_shapes=[
            pltpu.VMEM(key_pool.shape, bf16),
            pltpu.VMEM(key_pool.shape, bf16),
            pltpu.SMEM((devices,), jnp.int32),
            pltpu.VMEM((tokens, width), bf16),
            pltpu.VMEM((tokens, width), bf16),
            pltpu.VMEM((tokens, width), bf16),
            pltpu.VMEM((2, chunks, rows, HEAD_WIDTH), bf16),
            pltpu.VMEM((HEAD_WIDTH, count), bf16),
            pltpu.VMEM((HEAD_WIDTH, tokens), bf16),
            pltpu.VMEM((HEAD_WIDTH, tokens), bf16),
            pltpu.VMEM((HEAD_WIDTH, tokens), bf16),
            pltpu.VMEM((HEAD_WIDTH, tokens), bf16),
            pltpu.VMEM((count, tokens), f32),
            pltpu.VMEM((count, tokens), f32),
            pltpu.VMEM((count, tokens), f32),
            pltpu.VMEM((count, tokens), f32),
            pltpu.VMEM((rings, 2 * rows, query_rows), bf16),
            pltpu.VMEM((rings, 2 * rows, query_rows), bf16),
            pltpu.VMEM((query_rows, HEAD_WIDTH), bf16),
            pltpu.VMEM((query_rows, HEAD_WIDTH), bf16),
            pltpu.VMEM((rings, 2, SLOTS, rows, HEAD_WIDTH), f32),
            pltpu.VMEM((x_count, rings, 2 * ROWS, HEAD_WIDTH), bf16),
            pltpu.VMEM((devices, 2 * ROWS, HEAD_WIDTH), bf16),
            pltpu.VMEM((rings - 2, 2, rows, HEAD_WIDTH), bf16),
            pltpu.VMEM((rings - 2, 2, rows, HEAD_WIDTH), bf16),
            pltpu.VMEM((z_copies, rows, HEAD_WIDTH), bf16),
            pltpu.VMEM((z_copies, rows, HEAD_WIDTH), bf16),
            pltpu.VMEM((2, rows, HEAD_WIDTH), f32),
            pltpu.VMEM((rings, 2 * ROWS, HEAD_WIDTH), bf16),
            pltpu.VMEM((devices, 2 * ROWS, HEAD_WIDTH), bf16),
            pltpu.VMEM((x_count, rings, 2 * ROWS, HEAD_WIDTH), bf16),
            dma((4,)),
            dma,
            dma,
            dma((gathers,)),
            dma((gathers,)),
            dma((rings - 2,)),
            dma((rings - 2,)),
            dma((z_copies,)),
            dma((z_copies,)),
            dma,
            dma,
        ],
        compiler_params=pltpu.CompilerParams(
            collective_id=0, has_side_effects=True, vmem_limit_bytes=60 * 2**20
        ),
    )(tables, lengths, query, upstream, key_pool, value_pool)


def shards(query, output_gradient, prompt_key_pool, prompt_value_pool, block_tables, lengths):
    grad_query, grad_key, grad_value = gradients(
        block_tables, lengths, query[0], output_gradient[0], prompt_key_pool, prompt_value_pool
    )
    return grad_query[None], grad_key, grad_value


def solution(mesh):
    placed = (
        P("resp", None, "kvh"),
        P("resp", None, "kvh"),
        P("resp", "kvh", None),
        P("resp", "kvh", None),
        P(),
        P("resp"),
    )
    return jax.shard_map(
        shards,
        mesh=mesh,
        in_specs=placed,
        out_specs=(P("resp", None, "kvh"), P("resp", "kvh", None), P("resp", "kvh", None)),
        check_vma=False,
    )
```

time: 95.6 us -> 91 us (0.952)
  Pallas kernels: 87.2 us -> 84.4 us
  local copies, waits for them, and re-layouts: 6.86 us -> 5.04 us
    pallas_call x1, Pallas kernels: 87.2 us -> 84.4 us  [gradients(): pl.pallas_call(functools.partial(whole_kernel, share, page_count), out_sh...]
    unnamed x12 -> x8, local copies, waits for them, and re-layouts: 6.86 us -> 5.04 us
where the time goes in v3:
time: 91 us; the launch traced here: 90.7 us
  Pallas kernels  84.4 us (93%)
  local copies, waits for them, and re-layouts  5.04 us (6%)
  between operations  1.3 us (1%)
    pallas_call x1, Pallas kernels, gradients(): pl.pallas_call(functools.partial(whole_kernel, share, page_count), out_sh...  84.4 us
    unnamed x8, local copies, waits for them, and re-layouts  5.04 us

profile of v3, /device:TPU:1, one launch (start us, length us, event | category | flops | bytes accessed | tf_op | source)
XLA Modules:
  0.0 90.7 jit_solution(10501998208223154948)
XLA Ops:
  1.3 1.4 %copy.9.tables = s32[32,16]{1,0:T(8,128)} copy(s32[32,16]{0,1:T(8,128)} %param.10) | data formatting | bytes 4096 | tf_op args[4]
  2.7 84.4 %shard_map.85 = (bf16[256,1024]{1,0:T(8,128)(2,1)}, f32[4,16,1024]{2,1,0:T(8,128)}, f32[4,16,1024]{2,1,0:T(8,128)}) custom-call(s32[32,16]{1,0:T(8,128)} %copy.9.tables, s32[1]{0:T(128)S(6)} %copy.13.lengths, bf16[256,1024]{1,0:T(8,128)(2,1)} %bitcast.3, bf16[256,1024]{1,0:T(8,128)(2,1)} %bitcast.4, bf16[4,16,1024]{2,1,0:T(8,128)(2,1)} %key_hbm.1, ...), custom_call_target="tpu_custom_call" | custom-call | tf_op jit(solution)/shard_map/pallas_call | solution.py:439
  87.1 0.0 copy-start.1
  87.1 1.9 %copy.14 = bf16[1,256,1024]{2,1,0:T(8,128)(2,1)} copy(bf16[1,256,1024]{2,1,0:T(8,128)(2,1)} %bitcast.5) | data formatting | bytes 1048576
  89.0 0.0 copy-done.1
  89.0 0.0 copy-start
  89.0 0.7 copy.15
  89.7 0.3 copy-done
  90.0 0.7 copy.16
Async XLA Ops:
  87.1 1.9 %copy-start.1 = (f32[4,16,1024]{2,1,0:T(8,128)S(1)}, f32[4,16,1024]{2,1,0:T(8,128)}, u32[]{:S(2)}) copy-start(f32[4,16,1024]{2,1,0:T(8,128)} %get-tuple-element.13) | copy-start | bytes 786436
  89.0 1.0 %copy-start = (f32[4,16,1024]{2,1,0:T(8,128)S(1)}, f32[4,16,1024]{2,1,0:T(8,128)}, u32[]{:S(2)}) copy-start(f32[4,16,1024]{2,1,0:T(8,128)} %get-tuple-element.14) | copy-start | bytes 786436

commit v4 on v3

--- a/solution.py
+++ b/solution.py
@@ -32,7 +32,7 @@
 def local_slots(tables, prompt, own, share, pages):
     first, second, count = jnp.int32(-1), jnp.int32(-1), jnp.int32(0)
     for j in range(pages):
-        page = tables[prompt * share, j]
+        page = tables[j, prompt * share]
         hit = (page // PAGES_DEV) == own
         local = lax.rem(page, PAGES_DEV)
         first = jnp.where(hit & (count == 0), local, first)
@@ -42,7 +42,7 @@
 
 
 def prompt_owners(tables, prompt, share, pages):
-    held = [tables[prompt * share, j] // PAGES_DEV for j in range(pages)]
+    held = [tables[j, prompt * share] // PAGES_DEV for j in range(pages)]
     ranks = []
     for j in range(pages):
         below = jnp.int32(0)
@@ -60,15 +60,18 @@
 
 
 def spread_peers(own_x, own_z, head, rings, x_count):
+    def around(n, middle, size):
+        return mod(middle + (1 - 2 * lax.rem(n, 2)) * ((n + 1) // 2), size)
+
     def target(i):
-        dx, dh = i // rings, lax.rem(i, rings)
+        dx, dh = around(lax.rem(i, x_count), x_count // 2, x_count), around(i // x_count, rings // 2 + 1, rings)
         x = lax.rem(own_x + dx, x_count)
         h = lax.rem(head + dh, rings)
         z = mod(own_z - dh + 1, rings)
         return x, h, z
 
     def origin(i):
-        dx, dk = i // rings, lax.rem(i, rings)
+        dx, dk = around(lax.rem(i, x_count), x_count // 2, x_count), around(i // x_count, rings // 2 - 1, rings)
         x = lax.rem(own_x + dx, x_count)
         k = lax.rem(head + dk, rings)
         z = mod(own_z - dk - 1, rings)
@@ -177,9 +180,9 @@
         grads[pair, part] = value.reshape(SLOTS, -1, HEAD_WIDTH)
 
 
-def whole_kernel(share, page_count, tables, lengths, query_hbm, upstream_hbm, key_hbm, value_hbm,
+def whole_kernel(share, page_count, tables_hbm, lengths, query_hbm, upstream_hbm, key_hbm, value_hbm,
                  grad_query_hbm, grad_key, grad_value,
-                 key_pool, value_pool, ranks, query, upstream, grad_query, pages, keys_t, query_a, upstream_a,
+                 tables, key_pool, value_pool, ranks, query, upstream, grad_query, pages, keys_t, query_a, upstream_a,
                  query_b, upstream_b, score_a, slope_a, score_b, slope_b, soft, slopes,
                  query_s, upstream_s, grads, stage, recv, x_out, x_in, z_out, z_in, total, packed, back_stage, back,
                  copy_sem, spread_send, spread_recv, send_sem, recv_sem, x_send, x_recv, z_send, z_recv,
@@ -200,7 +203,8 @@
     loads = [
         pltpu.make_async_copy(source, place, copy_sem.at[n])
         for n, (source, place) in enumerate(
-            ((key_hbm, key_pool), (value_hbm, value_pool), (query_hbm, query), (upstream_hbm, upstream))
+            ((key_hbm, key_pool), (value_hbm, value_pool), (query_hbm, query), (upstream_hbm, upstream),
+             (tables_hbm, tables))
         )
     ]
     for load in loads:
@@ -218,6 +222,7 @@
     for peer in neighbours:
         pl.semaphore_signal(barrier, inc=1, device_id=(peer, head), device_id_type=MESH)
 
+    loads[4].wait()
     picked = []
     for prompt in range(x_count // 2):
         picked += local_slots(tables, prompt, own, share, page_count)
@@ -422,7 +427,7 @@
     devices = lax.axis_size("resp")
     x_count = devices // rings
     share = 2 * rings
-    page_count = tables.shape[1]
+    page_count = tables.shape[0]
     tokens, width = query.shape
     rows = rings * ROWS
     chunks = SLOTS * rings
@@ -439,9 +444,10 @@
     return pl.pallas_call(
         functools.partial(whole_kernel, share, page_count),
         out_shape=(jax.ShapeDtypeStruct(query.shape, bf16), out, out),
-        in_specs=[smem, smem, anywhere, anywhere, anywhere, anywhere],
+        in_specs=[anywhere, smem, anywhere, anywhere, anywhere, anywhere],
         out_specs=(anywhere, vmem, vmem),
         scratch_shapes=[
+            pltpu.SMEM(tables.shape, jnp.int32),
             pltpu.VMEM(key_pool.shape, bf16),
             pltpu.VMEM(key_pool.shape, bf16),
             pltpu.SMEM((devices,), jnp.int32),
@@ -473,7 +479,7 @@
             pltpu.VMEM((rings, 2 * ROWS, HEAD_WIDTH), bf16),
             pltpu.VMEM((devices, 2 * ROWS, HEAD_WIDTH), bf16),
             pltpu.VMEM((x_count, rings, 2 * ROWS, HEAD_WIDTH), bf16),
-            dma((4,)),
+            dma((5,)),
             dma,
             dma,
             dma((gathers,)),
@@ -493,7 +499,7 @@
 
 def shards(query, output_gradient, prompt_key_pool, prompt_value_pool, block_tables, lengths):
     grad_query, grad_key, grad_value = gradients(
-        block_tables, lengths, query[0], output_gradient[0], prompt_key_pool, prompt_value_pool
+        block_tables.T, lengths, query[0], output_gradient[0], prompt_key_pool, prompt_value_pool
     )
     return grad_query[None], grad_key, grad_value
 

time: 91 us -> 86.3 us (0.948)
  Pallas kernels: 84.4 us -> 81.2 us
  local copies, waits for them, and re-layouts: 5.04 us -> 3.66 us
    pallas_call x1, Pallas kernels: 84.4 us -> 81.2 us  [gradients(): pl.pallas_call(functools.partial(whole_kernel, share, page_count), out_sh...]
    unnamed x8 -> x7, local copies, waits for them, and re-layouts: 5.04 us -> 3.66 us
where the time goes in v4:
time: 86.3 us; the launch traced here: 86.1 us
  Pallas kernels  81.2 us (94%)
  local copies, waits for them, and re-layouts  3.66 us (4%)
  between operations  1.3 us (2%)
    pallas_call x1, Pallas kernels, gradients(): pl.pallas_call(functools.partial(whole_kernel, share, page_count), out_sh...  81.2 us
    unnamed x7, local copies, waits for them, and re-layouts  3.66 us

profile of v4, /device:TPU:1, one launch (start us, length us, event | category | flops | bytes accessed | tf_op | source)
XLA Modules:
  0.0 86.1 jit_solution(14903635967624514871)
XLA Ops:
  1.3 81.2 %shard_map.85 = (bf16[256,1024]{1,0:T(8,128)(2,1)}, f32[4,16,1024]{2,1,0:T(8,128)}, f32[4,16,1024]{2,1,0:T(8,128)}) custom-call(s32[16,32]{1,0:T(8,128)} %bitcast.7, s32[1]{0:T(128)S(6)} %copy.12.lengths, bf16[256,1024]{1,0:T(8,128)(2,1)} %bitcast.4, bf16[256,1024]{1,0:T(8,128)(2,1)} %bitcast.5, bf16[4,16,1024]{2,1,0:T(8,128)(2,1)} %key_hbm.1, ...), custom_call_target="tpu_custom_call" | custom-call | tf_op jit(solution)/shard_map/pallas_call | solution.py:444
  82.4 0.0 copy-start.1
  82.5 1.9 %copy.13 = bf16[1,256,1024]{2,1,0:T(8,128)(2,1)} copy(bf16[1,256,1024]{2,1,0:T(8,128)(2,1)} %bitcast.6) | data formatting | bytes 1048576
  84.4 0.0 copy-done.1
  84.4 0.0 copy-start
  84.4 0.7 copy.14
  85.1 0.3 copy-done
  85.4 0.7 copy.15
Async XLA Ops:
  82.4 1.9 %copy-start.1 = (f32[4,16,1024]{2,1,0:T(8,128)S(1)}, f32[4,16,1024]{2,1,0:T(8,128)}, u32[]{:S(2)}) copy-start(f32[4,16,1024]{2,1,0:T(8,128)} %get-tuple-element.13) | copy-start | bytes 786436
  84.4 1.0 %copy-start = (f32[4,16,1024]{2,1,0:T(8,128)S(1)}, f32[4,16,1024]{2,1,0:T(8,128)}, u32[]{:S(2)}) copy-start(f32[4,16,1024]{2,1,0:T(8,128)} %get-tuple-element.14) | copy-start | bytes 786436

commit v5 on v4

--- a/solution.py
+++ b/solution.py
@@ -420,6 +420,41 @@
     pltpu.make_async_copy(stage, stage, spread_send).wait()
     pltpu.make_async_copy(back_stage, back_stage, back_send).wait()
     store_query.wait()
+
+
+def settle_kernel(pieces, count, *refs):
+    sources, places, held = refs[:count], refs[count:2 * count], refs[2 * count:3 * count]
+    arrive, leave = refs[-2:]
+    inward, outward = [], []
+    for source, place, local in zip(sources, places, held):
+        rows = source.shape[0] // pieces
+        for n in range(pieces):
+            part = pl.ds(n * rows, rows)
+            slot = len(inward)
+            inward.append(pltpu.make_async_copy(source.at[part], local.at[part], arrive.at[slot]))
+            outward.append(pltpu.make_async_copy(local.at[part], place.at[part], leave.at[slot]))
+    for copy in inward:
+        copy.start()
+    for first, second in zip(inward, outward):
+        first.wait()
+        second.start()
+    for copy in outward:
+        copy.wait()
+
+
+def settled(arrays):
+    pieces = 2
+    anywhere = pl.BlockSpec(memory_space=pl.ANY)
+    copies = pieces * len(arrays)
+    return pl.pallas_call(
+        functools.partial(settle_kernel, pieces, len(arrays)),
+        out_shape=tuple(jax.ShapeDtypeStruct(a.shape, a.dtype) for a in arrays),
+        in_specs=[anywhere] * len(arrays),
+        out_specs=(anywhere,) * len(arrays),
+        scratch_shapes=[pltpu.VMEM(a.shape, a.dtype) for a in arrays]
+        + [pltpu.SemaphoreType.DMA((copies,)), pltpu.SemaphoreType.DMA((copies,))],
+        compiler_params=pltpu.CompilerParams(vmem_limit_bytes=60 * 2**20),
+    )(*arrays)
 
 
 def gradients(tables, lengths, query, upstream, key_pool, value_pool):
@@ -498,8 +533,8 @@
 
 
 def shards(query, output_gradient, prompt_key_pool, prompt_value_pool, block_tables, lengths):
-    grad_query, grad_key, grad_value = gradients(
-        block_tables.T, lengths, query[0], output_gradient[0], prompt_key_pool, prompt_value_pool
+    grad_query, grad_key, grad_value = settled(
+        gradients(block_tables.T, lengths, query[0], output_gradient[0], prompt_key_pool, prompt_value_pool)
     )
     return grad_query[None], grad_key, grad_value
 

time: 86.3 us -> 84.6 us (0.980)
  local copies, waits for them, and re-layouts: 3.66 us -> 0 us
  Pallas kernels: 81.2 us -> 83.2 us
    unnamed x7 -> x0, local copies, waits for them, and re-layouts: 3.66 us -> none
    pallas_call x0 -> x1, Pallas kernels: none -> 2.01 us  [settled(): pl.pallas_call(functools.partial(settle_kernel, pieces, len(arrays)), out...]
where the time goes in v5:
time: 84.6 us; the launch traced here: 84.5 us
  Pallas kernels  83.2 us (98%)
  between operations  1.29 us (2%)
    pallas_call x1, Pallas kernels, gradients(): pl.pallas_call(functools.partial(whole_kernel, share, page_count), out_sh...  81.2 us
    pallas_call x1, Pallas kernels, settled(): pl.pallas_call(functools.partial(settle_kernel, pieces, len(arrays)), out...  2.01 us

profile of v5, /device:TPU:1, one launch (start us, length us, event | category | flops | bytes accessed | tf_op | source)
XLA Modules:
  0.0 84.5 jit_solution(11720917568437246523)
XLA Ops:
  1.3 81.2 %shard_map.85 = (bf16[256,1024]{1,0:T(8,128)(2,1)}, f32[4,16,1024]{2,1,0:T(8,128)}, f32[4,16,1024]{2,1,0:T(8,128)}) custom-call(s32[16,32]{1,0:T(8,128)} %bitcast.6, s32[1]{0:T(128)S(6)} %copy.9.lengths, bf16[256,1024]{1,0:T(8,128)(2,1)} %bitcast.4, bf16[256,1024]{1,0:T(8,128)(2,1)} %bitcast.5, bf16[4,16,1024]{2,1,0:T(8,128)(2,1)} %key_hbm.1, ...), custom_call_target="tpu_custom_call" | custom-call | tf_op jit(solution)/shard_map/pallas_call | solution.py:479
  82.4 2.0 %shard_map.86 = (bf16[256,1024]{1,0:T(8,128)(2,1)}, f32[4,16,1024]{2,1,0:T(8,128)}, f32[4,16,1024]{2,1,0:T(8,128)}) custom-call(bf16[256,1024]{1,0:T(8,128)(2,1)} %get-tuple-element.9.refs_0_, f32[4,16,1024]{2,1,0:T(8,128)} %get-tuple-element.10.refs_1_, f32[4,16,1024]{2,1,0:T(8,128)} %get-tuple-element.11.refs_2_), custom_call_target="tpu_custom_call" | custom-call | tf_op jit(solution)/shard_map/pallas_call | solution.py:449
